TPU v7x, 256 devices: a whole 4x4x8 slice. The times are simulated.
256 devices in a mesh: row: 32 (over y, x, core), col: 8 (over z).
Axes of the slice: x: 4, y: 4, z: 8, core: 2. Of those that a mesh axis runs over, the one named last changes fastest.
Arguments:
- a_tiles: bfloat16 [32, 2048, 128, 128], P('row', 'col'), may hold values from -1.25 to 1.25
- a_rows: int32 [32, 2048], P('row', 'col'), may hold values from 0 to 47
- a_cols: int32 [32, 2048], P('row', 'col'), may hold values from 0 to 47
- a_count: int32 [32, 8], P('row', 'col'), may hold values from 64 to 256, as said below
- p_panels: bfloat16 [4096, 128, 256], P(('row', 'col')), may hold values from -1.25 to 1.25
Outputs:
- coarse_bands: float32 [8, 256, 768], P('col', 'row')
Inputs may be any that keep to these rules, and one draw needn't show every extreme that they name: Only the first a_count slots of a device are live; the count reaches 256 on some devices in every draw.
All inputs are finite; a program needn't handle non-finite values.
Results may differ from a plain program's by a relative error of at most 0.0029.
Values may be sent and summed in bfloat16 or wider, within the bound.
No kernel may reach another device: no remote copies, remote signals or barrier semaphores. Data moves between devices by JAX's collectives and lax.ppermute only.
A program may use at most 64 MiB of HBM per device.

v0:
```python
import jax
import jax.numpy as jnp
from jax import lax
from jax.sharding import PartitionSpec as P


def with_halo(block, sides, width):
    for axis, dim in sides:
        count = lax.axis_size(axis)
        forward = [(i, i + 1) for i in range(count - 1)]
        backward = [(target, source) for source, target in forward]
        low = lax.ppermute(
            lax.slice_in_dim(block, block.shape[dim] - width, None, axis=dim), axis, forward
        )
        high = lax.ppermute(lax.slice_in_dim(block, 0, width, axis=dim), axis, backward)
        block = jnp.concatenate([low, block, high], axis=dim)
    return block


def from_behind(value, axis, steps):
    count = lax.axis_size(axis)
    leading, last = (max(0, -steps), min(count, count - steps))
    return lax.ppermute(value, axis, [(source, source + steps) for source in range(leading, last)])


def local(a_tiles, a_rows, a_cols, a_count, p_panels):
    panel_count = p_panels.shape[0]
    band_width = p_panels.shape[2]
    slot_count = a_tiles.shape[1]
    group_size = min(16, slot_count)
    col_side = with_halo(p_panels, (("row", 0),), panel_count)
    row_side = with_halo(p_panels, (("col", 0),), panel_count)
    a_local = a_tiles[0]
    row_index = a_rows[0]
    col_index = a_cols[0]
    live_count = a_count[0, 0]

    def accumulate(group_index, partial_sums):
        first_slot = group_index * group_size
        tile_group = lax.dynamic_slice_in_dim(a_local, first_slot, group_size, 0)
        row_ids = lax.dynamic_slice_in_dim(row_index, first_slot, group_size, 0)
        col_ids = lax.dynamic_slice_in_dim(col_index, first_slot, group_size, 0)
        right_panels = jnp.take(col_side, col_ids, axis=0)
        applied = jnp.einsum(
            "tab,tbw->taw", tile_group, right_panels, preferred_element_type=jnp.float32
        ).astype(jnp.bfloat16)
        left_panels = jnp.take(row_side, row_ids, axis=0)
        contribution = jnp.einsum(
            "tkm,tkn->tmn", left_panels, applied, preferred_element_type=jnp.float32
        )
        in_use = first_slot + jnp.arange(group_size) < live_count
        band_offset = row_ids // panel_count
        selector = ((band_offset[:, None] == jnp.arange(3)[None, :]) & in_use[:, None]).astype(
            jnp.float32
        )
        return partial_sums + jnp.einsum(
            "to,tmn->omn", selector, contribution, precision=lax.Precision.HIGHEST
        )

    group_total = (live_count + group_size - 1) // group_size
    partial_sums = lax.fori_loop(
        0, group_total, accumulate, jnp.zeros((3, band_width, band_width), jnp.float32)
    )
    from_lower = from_behind(partial_sums[2], "col", 1)
    from_upper = from_behind(partial_sums[0], "col", -1)
    stacked = jnp.concatenate([from_lower, partial_sums[1], from_upper], axis=1)
    summed = lax.psum_scatter(stacked, "row", scatter_dimension=0, tiled=True)
    return summed[None]


def solution(mesh):
    in_specs = (
        P("row", "col", None, None),
        P("row", "col"),
        P("row", "col"),
        P("row", "col"),
        P(("row", "col"), None, None),
    )
    out_specs = P("col", "row", None)
    return jax.shard_map(local, mesh=mesh, in_specs=in_specs, out_specs=out_specs, check_vma=False)
```

profile of v0, /device:TPU:1, one launch (start us, length us, event | category | flops | bytes accessed | tf_op | source)
XLA Modules:
  0.0 417.2 jit_solution(8033869679143193404)
XLA Ops:
  6.5 4.4 %collective-permute-start = (bf16[16,128,256]{2,1,0:T(8,128)(2,1)}, bf16[16,128,256]{2,1,0:T(8,128)(2,1)S(1)}, u32[]{:S(2)}, u32[]{:S(2)}) collective-permute-start(bf16[16,128,256]{2,1,0:T(8,128)(2,1)} %param.13), channel_id=1, source_target_pairs={{0,1},{1,2},{2,3},{3,4},{4,5},{5,6},{6,7},{8,9},{9,10},{10,11},{11... | collective-permute-start | bytes 3145736 | tf_op jit(solution)/shard_map/ppermute | solution.py:12
  12.3 4.0 collective-permute-start.2
  18.9 14.2 %collective-permute-done = bf16[16,128,256]{2,1,0:T(8,128)(2,1)S(1)} collective-permute-done((bf16[16,128,256]{2,1,0:T(8,128)(2,1)}, bf16[16,128,256]{2,1,0:T(8,128)(2,1)S(1)}, u32[]{:S(2)}, u32[]{:S(2)}) %collective-permute-start) | collective-permute-done | bytes 1048608 | tf_op jit(solution)/shard_map/ppermute | solution.py:12
  33.0 4.0 collective-permute-done.1
  37.0 4.2 %fusion.26 = (bf16[48,128,256]{2,1,0:T(8,128)(2,1)}, bf16[48,128,256]{2,1,0:T(8,128)(2,1)}) fusion(bf16[16,128,256]{2,1,0:T(8,128)(2,1)} %param.13, bf16[16,128,256]{2,1,0:T(8,128)(2,1)} %collective-permute-done.3, bf16[16,128,256]{2,1,0:T(8,128)(2,1)S(1)} %collective-permute-done.2, bf16[16,128,256]{2,1,0:T(8,128)(2,1)S(1)} %collective-permute-done.1, ...), kind=kLoop, calls=%fused_computation.34 | loop fusion | flops 6291456 | bytes 11534336 | tf_op jit(solution)/shard_map/concatenate | solution.py:16
  41.4 84.0 %while.12 = (s32[]{:T(128)}, f32[3,256,256]{2,0,1:T(4,128)S(1)}, s32[]{:T(128)}, s32[256]{0:T(256)S(1)}, s32[]{:T(128)}, /*index=5*/bf16[48,128,256]{2,1,0:T(8,1...) while((s32[]{:T(128)}, f32[3,256,256]{2,0,1:T(4,128)S(1)}, ...), condition=%wide.region_1.3_spmd, body=%wide.region_0.2_spmd.sunk | while | flops 442174016 | bytes 16786400 | solution.py:61
  44.1 2.5 gather_fusion.1
  46.6 4.1 fusion.39
  51.4 6.9 %fusion.40 = f32[3,256,256]{2,0,1:T(4,128)S(1)} fusion(f32[3,256,256]{2,0,1:T(4,128)S(1)} %get-tuple-element.231, f32[16,256,256]{2,1,0:T(8,128)} %fusion.39, s32[16]{0:T(128)S(1)} %and_select_fusion.2, pred[16]{0:T(512)(128)(4,1)S(1)} %add_compare_fusion.2), kind=kOutput, calls=%fused_computation.5.clone.1 | convolution fusion | flops 37945440 | bytes 5767248 | tf_op jit(solution)/shard_map/while/body/to,tmn->omn/dot_general | solution.py:56
  58.3 2.5 gather_fusion
  60.9 2.5 gather_fusion.1
  63.4 4.1 fusion.39
  68.2 6.9 %fusion.40 = f32[3,256,256]{2,0,1:T(4,128)S(1)} fusion(f32[3,256,256]{2,0,1:T(4,128)S(1)} %get-tuple-element.231, f32[16,256,256]{2,1,0:T(8,128)} %fusion.39, s32[16]{0:T(128)S(1)} %and_select_fusion.2, pred[16]{0:T(512)(128)(4,1)S(1)} %add_compare_fusion.2), kind=kOutput, calls=%fused_computation.5.clone.1 | convolution fusion | flops 37945440 | bytes 5767248 | tf_op jit(solution)/shard_map/while/body/to,tmn->omn/dot_general | solution.py:56
  75.2 2.5 gather_fusion
  80.2 4.1 fusion.39
  85.0 6.9 %fusion.40 = f32[3,256,256]{2,0,1:T(4,128)S(1)} fusion(f32[3,256,256]{2,0,1:T(4,128)S(1)} %get-tuple-element.231, f32[16,256,256]{2,1,0:T(8,128)} %fusion.39, s32[16]{0:T(128)S(1)} %and_select_fusion.2, pred[16]{0:T(512)(128)(4,1)S(1)} %add_compare_fusion.2), kind=kOutput, calls=%fused_computation.5.clone.1 | convolution fusion | flops 37945440 | bytes 5767248 | tf_op jit(solution)/shard_map/while/body/to,tmn->omn/dot_general | solution.py:56
  97.0 4.1 fusion.39
  101.8 6.9 %fusion.40 = f32[3,256,256]{2,0,1:T(4,128)S(1)} fusion(f32[3,256,256]{2,0,1:T(4,128)S(1)} %get-tuple-element.231, f32[16,256,256]{2,1,0:T(8,128)} %fusion.39, s32[16]{0:T(128)S(1)} %and_select_fusion.2, pred[16]{0:T(512)(128)(4,1)S(1)} %add_compare_fusion.2), kind=kOutput, calls=%fused_computation.5.clone.1 | convolution fusion | flops 37945440 | bytes 5767248 | tf_op jit(solution)/shard_map/while/body/to,tmn->omn/dot_general | solution.py:56
  113.8 4.1 fusion.39
  118.6 6.9 %fusion.40 = f32[3,256,256]{2,0,1:T(4,128)S(1)} fusion(f32[3,256,256]{2,0,1:T(4,128)S(1)} %get-tuple-element.231, f32[16,256,256]{2,1,0:T(8,128)} %fusion.39, s32[16]{0:T(128)S(1)} %and_select_fusion.2, pred[16]{0:T(512)(128)(4,1)S(1)} %add_compare_fusion.2), kind=kOutput, calls=%fused_computation.5.clone.1 | convolution fusion | flops 37945440 | bytes 5767248 | tf_op jit(solution)/shard_map/while/body/to,tmn->omn/dot_general | solution.py:56
  125.7 54.0 %collective-permute-start.4 = (f32[256,256]{1,0:T(8,128)S(1)}, f32[256,256]{1,0:T(8,128)S(1)}, u32[]{:S(2)}, u32[]{:S(2)}) collective-permute-start(f32[256,256]{1,0:T(8,128)S(1)} %get-tuple-element.150), channel_id=1, source_target_pairs={{0,1},{1,2},{2,3},{3,4},{4,5},{5,6},{6,7},{8,9},{9,10},{10,11},{11... | collective-permute-start | bytes 786440 | tf_op jit(solution)/shard_map/ppermute | solution.py:23
  181.0 2.6 collective-permute-done.4
  183.6 3.8 collective-permute-done.5
  188.4 221.9 %reduce-scatter.2.cloned.1.call-done = f32[8,768]{1,0:T(8,128)} async-done(((f32[256,768]{1,0:T(8,128)}), f32[8,768]{1,0:T(8,128)}) %reduce-scatter.2.cloned.1.call-update) | async-done | bytes 24592 | tf_op jit(solution)/shard_map/reduce_scatter | solution.py:67
  (46 shorter events, 25.0 us)
Async XLA Ops:
  6.5 403.8 %reduce-scatter.2.cloned.1.call-start = ((), (), s32[]{:S(2)}) async-start(), calls=%async_computation.1 | async-start | bytes 811008 | tf_op jit(solution)/shard_map/reduce_scatter | solution.py:67
  6.5 26.5 %collective-permute-start = (bf16[16,128,256]{2,1,0:T(8,128)(2,1)}, bf16[16,128,256]{2,1,0:T(8,128)(2,1)S(1)}, u32[]{:S(2)}, u32[]{:S(2)}) collective-permute-start(bf16[16,128,256]{2,1,0:T(8,128)(2,1)} %param.13), channel_id=1, source_target_pairs={{0,1},{1,2},{2,3},{3,4},{4,5},{5,6},{6,7},{8,9},{9,10},{10,11},{11... | collective-permute-start | bytes 3145736 | tf_op jit(solution)/shard_map/ppermute | solution.py:12
  11.0 26.1 %collective-permute-start.1 = (bf16[16,128,256]{2,1,0:T(8,128)(2,1)}, bf16[16,128,256]{2,1,0:T(8,128)(2,1)S(1)}, u32[]{:S(2)}, u32[]{:S(2)}) collective-permute-start(bf16[16,128,256]{2,1,0:T(8,128)(2,1)} %param.13), channel_id=1, source_target_pairs={{1,0},{2,1},{3,2},{4,3},{5,4},{6,5},{7,6},{9,8},{10,9},{11,10},{12... | collective-permute-start | bytes 3145736 | tf_op jit(solution)/shard_map/ppermute | solution.py:15
  12.3 24.8 %collective-permute-start.2 = (bf16[16,128,256]{2,1,0:T(8,128)(2,1)}, bf16[16,128,256]{2,1,0:T(8,128)(2,1)S(1)}, u32[]{:S(2)}, u32[]{:S(2)}) collective-permute-start(bf16[16,128,256]{2,1,0:T(8,128)(2,1)} %param.13), channel_id=1, source_target_pairs={{0,8},{8,16},{16,24},{24,32},{32,40},{40,48},{48,56},{56,64},{64,7... | collective-permute-start | bytes 3145736 | tf_op jit(solution)/shard_map/ppermute | solution.py:12
  16.2 20.8 %collective-permute-start.3 = (bf16[16,128,256]{2,1,0:T(8,128)(2,1)}, bf16[16,128,256]{2,1,0:T(8,128)(2,1)}, u32[]{:S(2)}, u32[]{:S(2)}) collective-permute-start(bf16[16,128,256]{2,1,0:T(8,128)(2,1)} %param.13), channel_id=1, source_target_pairs={{8,0},{16,8},{24,16},{32,24},{40,32},{48,40},{56,48},{64,56},{72,6... | collective-permute-start | bytes 3145736 | tf_op jit(solution)/shard_map/ppermute | solution.py:15
  18.8 22.6 %copy-start = (s32[1,256]{1,0:T(1,128)S(1)}, s32[1,256]{1,0:T(1,128)}, u32[]{:S(2)}) copy-start(s32[1,256]{1,0:T(1,128)} %param.10) | copy-start | bytes 3076
  18.8 22.6 %copy-start.1 = (s32[1,256]{1,0:T(1,128)S(1)}, s32[1,256]{1,0:T(1,128)}, u32[]{:S(2)}) copy-start(s32[1,256]{1,0:T(1,128)} %param.11) | copy-start | bytes 3076
  125.7 57.9 %collective-permute-start.4 = (f32[256,256]{1,0:T(8,128)S(1)}, f32[256,256]{1,0:T(8,128)S(1)}, u32[]{:S(2)}, u32[]{:S(2)}) collective-permute-start(f32[256,256]{1,0:T(8,128)S(1)} %get-tuple-element.150), channel_id=1, source_target_pairs={{0,1},{1,2},{2,3},{3,4},{4,5},{5,6},{6,7},{8,9},{9,10},{10,11},{11... | collective-permute-start | bytes 786440 | tf_op jit(solution)/shard_map/ppermute | solution.py:23
  179.7 7.8 %collective-permute-start.5 = (f32[256,256]{1,0:T(8,128)S(1)}, f32[256,256]{1,0:T(8,128)S(1)}, u32[]{:S(2)}, u32[]{:S(2)}) collective-permute-start(f32[256,256]{1,0:T(8,128)S(1)} %get-tuple-element.151), channel_id=1, source_target_pairs={{1,0},{2,1},{3,2},{4,3},{5,4},{6,5},{7,6},{9,8},{10,9},{11,10},{12... | collective-permute-start | bytes 786440 | tf_op jit(solution)/shard_map/ppermute | solution.py:23
Sparse Core Ops, SparseCore 0:
  188.6 221.7 reduce-scatter.1
where the time goes:
time: 421 us; the launch traced here: 417 us
  waiting for transfers between devices  247 us (59%)
  starting transfers between devices  66.9 us (16%)
  matrix products  54.6 us (13%)
  local copies, waits for them, and re-layouts  25.4 us (6%)
  between operations  14.2 us (3%)
  other arithmetic  9.29 us (2%)
    reduce_scatter x1, waiting for transfers between devices, local(): summed = lax.psum_scatter(stacked, 'row', scatter_dimension=0, tiled=True)  222 us
    ppermute x2, starting transfers between devices, from_behind(): lax.ppermute(value, axis, [(source, source + steps) for source in range(l...  55.3 us
    dot_general x5, matrix products, accumulate(): jnp.einsum('to,tmn->omn', selector, contribution, precision=lax.Precision...  34.3 us
    dot_general x5, matrix products, accumulate(): jnp.einsum('tkm,tkn->tmn', left_panels, applied, preferred_element_type=j...  20.3 us
    ppermute x2, waiting for transfers between devices, with_halo(): lax.ppermute(lax.slice_in_dim(block, block.shape[dim] - width, None, axis...  14.2 us
    gather x5, local copies, waits for them, and re-layouts, accumulate(): left_panels = jnp.take(row_side, row_ids, axis=0)  12.5 us
    gather x5, local copies, waits for them, and re-layouts, accumulate(): right_panels = jnp.take(col_side, col_ids, axis=0)  12.5 us
  transfers between devices with their start and end apart: 7, of which 5 were waited for; matrix products, arithmetic and copies ran while one was open for 0% of the time, Pallas kernels for 0%

commit v1 on v0

v1 whole, which is shorter than its diff:
```python
import functools

import jax
import jax.numpy as jnp
from jax import lax
from jax.experimental import pallas as pl
from jax.experimental.pallas import tpu as pltpu
from jax.sharding import PartitionSpec as P

BF = jnp.bfloat16
F32 = jnp.float32
PANELS = 16
TILE = 128
BAND = 256
SLOTS = 256
UNROLL = 8
RING = 4
LIST = SLOTS + UNROLL
ANY = pl.BlockSpec(memory_space=pl.ANY)
SM = pl.BlockSpec(memory_space=pltpu.SMEM)
VM = pl.BlockSpec(memory_space=pltpu.VMEM)
X, Y = 4, 4


def vmem(mib):
    return pltpu.CompilerParams(vmem_limit_bytes=mib * 2**20)


def cost(flops, nbytes):
    return pl.CostEstimate(flops=flops, bytes_accessed=nbytes, transcendentals=0)


def plan_kernel(core, rows, cols, count, codes, counts):
    partner = jnp.where(core[0] == 0, 2, 0)

    def put(t, pos):
        n0, n1 = pos
        r, c = rows[0, t], cols[0, t]
        q = lax.div(c, PANELS)
        k = c - q * PANELS
        first = (q == 1) | (q == partner)
        at = jnp.where(first, n0, LIST + n1)
        codes[at] = t * 4096 + r * 64 + jnp.where(q == partner, k + PANELS, k)
        return jnp.where(first, n0 + 1, n0), jnp.where(first, n1, n1 + 1)

    n0, n1 = lax.fori_loop(0, count[0, 0], put, (jnp.int32(0), jnp.int32(0)))
    counts[0] = n0
    counts[1] = n1
    for i in range(UNROLL):
        codes[n0 + i] = 3 * PANELS * 64
        codes[LIST + n1 + i] = 3 * PANELS * 64


def plan(core, rows, cols, count):
    return pl.pallas_call(
        plan_kernel,
        out_shape=(
            jax.ShapeDtypeStruct((2 * LIST,), jnp.int32),
            jax.ShapeDtypeStruct((2,), jnp.int32),
        ),
        in_specs=[SM] * 4,
        out_specs=(SM, SM),
        name="plan",
        cost_estimate=cost(10**9, 10**4),
    )(core, rows, cols, count)


def apply_tiles(which, codes, counts, a_hbm, panels, sums, cbuf, abuf, csem, asem, prepare):
    base = which * LIST
    groups = lax.div(counts[which] + UNROLL - 1, UNROLL)
    loads = [
        pltpu.make_async_copy(p, cbuf.at[pl.ds(PANELS * i, PANELS)], csem.at[i])
        for i, p in enumerate(panels)
    ]
    for load in loads:
        load.start()

    def fetch(g):
        place = lax.rem(g, RING) * UNROLL
        for u in range(UNROLL):
            t = lax.div(codes[base + g * UNROLL + u], 4096)
            pltpu.make_async_copy(a_hbm.at[0, t], abuf.at[place + u], asem.at[place + u]).start()

    for g in range(RING - 1):
        @pl.when(g < groups)
        def _():
            fetch(g)

    prepare()
    for load in loads:
        load.wait()

    def step(g, carry):
        @pl.when(g + RING - 1 < groups)
        def _():
            fetch(g + RING - 1)

        place = lax.rem(g, RING) * UNROLL
        for u in range(UNROLL):
            pltpu.make_async_copy(a_hbm.at[0, 0], abuf.at[place + u], asem.at[place + u]).wait()
        applied, rows = [], []
        for u in range(UNROLL):
            code = codes[base + g * UNROLL + u]
            rows.append(lax.rem(lax.div(code, 64), 64))
            product = jnp.dot(
                abuf[place + u], cbuf[lax.rem(code, 64)], preferred_element_type=F32
            )
            applied.append(product.astype(BF).astype(F32))
        for u in range(UNROLL):
            sums[rows[u]] += applied[u]
        return carry

    lax.fori_loop(0, groups, step, 0)


def first_kernel(codes, counts, a_hbm, own, partner, sums, cbuf, abuf, csem, asem):
    def clear():
        def zero(i, carry):
            sums[i] = jnp.zeros((TILE, BAND), F32)
            return carry

        lax.fori_loop(0, 3 * PANELS + 1, zero, 0)

    apply_tiles(0, codes, counts, a_hbm, (own, partner), sums, cbuf, abuf, csem, asem, clear)


def second_kernel(codes, counts, a_hbm, other, before, turned, sums, cbuf, abuf, csem, asem, ssem):
    def load_sums():
        copy = pltpu.make_async_copy(before, sums, ssem)
        copy.start()
        copy.wait()

    apply_tiles(1, codes, counts, a_hbm, (other,), sums, cbuf, abuf, csem, asem, load_sums)
    for k in range(3 * PANELS):
        lanes = pl.ds((k % PANELS) * TILE, TILE)
        turned[k // PANELS, :, lanes] = sums[k].T.astype(BF)


SUMS = (3 * PANELS + 1, TILE, BAND)


def scratch(panel_sets):
    return [
        pltpu.VMEM((panel_sets * PANELS, TILE, BAND), BF),
        pltpu.VMEM((RING * UNROLL, TILE, TILE), BF),
        pltpu.SemaphoreType.DMA((panel_sets,)),
        pltpu.SemaphoreType.DMA((RING * UNROLL,)),
    ]


def first_sums(codes, counts, a_tiles, own, partner):
    return pl.pallas_call(
        first_kernel,
        out_shape=jax.ShapeDtypeStruct(SUMS, F32),
        in_specs=[SM, SM, ANY, ANY, ANY],
        out_specs=VM,
        scratch_shapes=scratch(2),
        compiler_params=vmem(24),
        name="first_sums",
        cost_estimate=cost(10 * 10**9, 16 * 2**20),
    )(codes, counts, a_tiles, own, partner)


def second_sums(codes, counts, a_tiles, other, before):
    return pl.pallas_call(
        second_kernel,
        out_shape=jax.ShapeDtypeStruct((3, BAND, PANELS * TILE), BF),
        in_specs=[SM, SM, ANY, ANY, ANY],
        out_specs=VM,
        scratch_shapes=[pltpu.VMEM(SUMS, F32)] + scratch(1) + [pltpu.SemaphoreType.DMA],
        compiler_params=vmem(24),
        name="second_sums",
        cost_estimate=cost(10 * 10**9, 16 * 2**20),
    )(codes, counts, a_tiles, other, before)


def couple_kernel(core, turned, low, own, high, out):
    me = core[0]
    for o, panels in enumerate((low, own, high)):
        rows = panels[...].reshape(PANELS * TILE, BAND)
        term = jnp.dot(turned[o], rows, preferred_element_type=F32).T
        lanes = pl.ds(o * BAND, BAND)
        for block in range(BAND // 8):
            y, x, c = block // (2 * X), (block // 2) % X, block % 2
            out[me ^ c, x, y, :, lanes] = term[block * 8:(block + 1) * 8]


def couple(core, turned, low, own, high):
    return pl.pallas_call(
        couple_kernel,
        out_shape=jax.ShapeDtypeStruct((2, X, Y, 8, 3 * BAND), F32),
        in_specs=[SM, VM, VM, VM, VM],
        out_specs=VM,
        compiler_params=vmem(24),
        name="couple",
        cost_estimate=cost(10**9, 6 * 2**20),
    )(core, turned, low, own, high)


def shift(value, axis, pairs):
    return lax.ppermute(value, axis, pairs)


def exchange_sum(value, place, pairs_of, kind):
    total = lax.dynamic_index_in_dim(value, place, 0, False)
    for k in range(1, value.shape[0]):
        there = lax.rem(place + k, value.shape[0])
        block = lax.dynamic_index_in_dim(value, there, 0, False).astype(kind)
        total = total + shift(block, "row", pairs_of(k)).astype(F32)
    return total


def at(y, x, core):
    return (y % Y * X + x % X) * 2 + core


PLACES = [(y, x, c) for y in range(Y) for x in range(X) for c in range(2)]


def along_x(k):
    return [(at(y, x, c), at(y, x + k, c)) for y, x, c in PLACES]


def along_y(k):
    return [(at(y, x, c), at(y + k, x, c)) for y, x, c in PLACES]


def local(a_tiles, a_rows, a_cols, a_count, p_panels):
    n_row, n_col = lax.axis_size("row"), lax.axis_size("col")
    row = lax.axis_index("row")
    core, x, y = row % 2, row // 2 % X, row // (2 * X)
    up = [(i, i + 1) for i in range(n_col - 1)]
    down = [(j, i) for i, j in up]
    pairs = [(i, i ^ 1) for i in range(n_row)]
    bridges = [(i, i + 1) for i in range(1, n_row - 1, 2)]
    bridges += [(j, i) for i, j in bridges]
    low = shift(p_panels, "col", up)
    high = shift(p_panels, "col", down)
    other = shift(p_panels, "row", bridges)
    partner = shift(p_panels, "row", pairs)
    core_id = core.astype(jnp.int32)[None]
    codes, counts = plan(core_id, a_rows, a_cols, a_count)
    before = first_sums(codes, counts, a_tiles, p_panels, partner)
    turned = second_sums(codes, counts, a_tiles, other, before)
    terms = couple(core_id, turned, low, p_panels, high)
    chip = terms[0] + shift(terms[1], "row", pairs)
    line = exchange_sum(chip.reshape(X, Y * 8, 3 * BAND), x, along_x, BF)
    rows = exchange_sum(line.reshape(Y, 8, 3 * BAND), y, along_y, F32)
    from_lower = shift(rows[:, 2 * BAND:], "col", up)
    from_upper = shift(rows[:, :BAND], "col", down)
    return jnp.concatenate([from_lower, rows[:, BAND:2 * BAND], from_upper], axis=1)[None]


def solution(mesh):
    in_specs = (
        P("row", "col", None, None),
        P("row", "col"),
        P("row", "col"),
        P("row", "col"),
        P(("row", "col"), None, None),
    )
    out_specs = P("col", "row", None)
    return jax.shard_map(local, mesh=mesh, in_specs=in_specs, out_specs=out_specs, check_vma=False)
```

time: 421 us -> 78.7 us (0.19)
  the two profiles are of different devices: /device:TPU:1 before, /device:TPU:128 now
where the time goes in v1:
time: 78.7 us; the launch traced here: 78.1 us
  starting transfers between devices  39.7 us (50%)
  waiting for transfers between devices  16.7 us (21%)
  Pallas kernels  14.3 us (18%)
  local copies, waits for them, and re-layouts  5.98 us (8%)
  between operations  0.82 us (1%)
    ppermute x13, starting transfers between devices, shift(): return lax.ppermute(value, axis, pairs)  39.7 us
    ppermute x13, waiting for transfers between devices, shift(): return lax.ppermute(value, axis, pairs)  16.7 us
    unnamed x10, local copies, waits for them, and re-layouts  5.9 us
    pallas_call x1, Pallas kernels, first_sums(): pl.pallas_call(first_kernel, out_shape=jax.ShapeDtypeStruct(SUMS, F32), i...  5.68 us
    pallas_call x1, Pallas kernels, second_sums(): pl.pallas_call(second_kernel, out_shape=jax.ShapeDtypeStruct((3, BAND, PA...  5.21 us
    pallas_call x1, Pallas kernels, plan(): pl.pallas_call(plan_kernel, out_shape=(jax.ShapeDtypeStruct((2 * LIST,),...  2.23 us
  transfers between devices with their start and end apart: 13, of which 9 were waited for; matrix products, arithmetic and copies ran while one was open for 0% of the time, Pallas kernels for 17%

profile of v1, /device:TPU:128, one launch (start us, length us, event | category | flops | bytes accessed | tf_op | source)
XLA Modules:
  0.0 78.1 jit_solution(600220168492690225)
XLA Ops:
  0.0 1.6 %collective-permute-start = (bf16[16,128,256]{2,1,0:T(8,128)(2,1)}, bf16[16,128,256]{2,1,0:T(8,128)(2,1)}, u32[]{:S(2)}, u32[]{:S(2)}) collective-permute-start(bf16[16,128,256]{2,1,0:T(8,128)(2,1)} %own.3), channel_id=1, source_target_pairs={{8,16},{24,32},{40,48},{56,64},{72,80},{88,96},{104,112},{120,128}... | collective-permute-start | bytes 3145736 | tf_op jit(solution)/shard_map/ppermute | solution.py:201
  1.6 2.9 %collective-permute-start.2 = (bf16[16,128,256]{2,1,0:T(8,128)(2,1)}, bf16[16,128,256]{2,1,0:T(8,128)(2,1)S(1)}, u32[]{:S(2)}, u32[]{:S(2)}) collective-permute-start(bf16[16,128,256]{2,1,0:T(8,128)(2,1)} %own.3), channel_id=1, source_target_pairs={{0,1},{1,2},{2,3},{3,4},{4,5},{5,6},{6,7},{8,9},{9,10},{10,11},{11... | collective-permute-start | bytes 3145736 | tf_op jit(solution)/shard_map/ppermute | solution.py:201
  4.6 4.1 %collective-permute-start.3 = (bf16[16,128,256]{2,1,0:T(8,128)(2,1)}, bf16[16,128,256]{2,1,0:T(8,128)(2,1)S(1)}, u32[]{:S(2)}, u32[]{:S(2)}) collective-permute-start(bf16[16,128,256]{2,1,0:T(8,128)(2,1)} %own.3), channel_id=1, source_target_pairs={{1,0},{2,1},{3,2},{4,3},{5,4},{6,5},{7,6},{9,8},{10,9},{11,10},{12... | collective-permute-start | bytes 3145736 | tf_op jit(solution)/shard_map/ppermute | solution.py:201
  9.4 2.2 %plan.1 = (s32[528]{0:T(1024)}, s32[2]{0:T(128)}) custom-call(s32[1]{0:T(128)} %bitcast.core, s32[1,256]{1,0:T(1,128)} %rows.1, s32[1,256]{1,0:T(1,128)} %cols.1, s32[1,1]{1,0:T(1,128)S(6)} %copy.6.count), custom_call_target="tpu_custom_call" | custom-call | flops 1000000000 | bytes 10000 | tf_op jit(solution)/shard_map/plan/pallas_call | solution.py:55
  11.6 1.2 %copy-done = bf16[16,128,256]{2,1,0:T(8,128)(2,1)S(1)} copy-done((bf16[16,128,256]{2,1,0:T(8,128)(2,1)S(1)}, bf16[16,128,256]{2,1,0:T(8,128)(2,1)}, u32[]{:S(2)}) %copy-start) | copy-done | bytes 1048600
  12.8 3.4 %copy-done.2 = bf16[1,256,128,128]{3,2,1,0:T(8,128)(2,1)S(1)} copy-done((bf16[1,256,128,128]{3,2,1,0:T(8,128)(2,1)S(1)}, bf16[1,256,128,128]{3,2,1,0:T(8,128)(2,1)}, u32[]{:S(2)}) %copy-start.2) | copy-done | bytes 8388632
  17.5 5.7 %first_sums.1.before = f32[49,128,256]{2,1,0:T(8,128)S(1)} custom-call(s32[528]{0:T(1024)S(1)} %copy-done.3, s32[2]{0:T(128)S(1)} %copy-done.4, bf16[1,256,128,128]{3,2,1,0:T(8,128)(2,1)S(1)} %copy-done.2, bf16[16,128,256]{2,1,0:T(8,128)(2,1)S(1)} %copy-done, bf16[16,128,256]{2,1,0:T(8,128)(2,1)} %collective-permute-done.1.partner), custom_call_target="tpu_custom_call" | custom-call | flops 10000000000 | bytes 16777216 | tf_op jit(solution)/shard_map/first_sums/pallas_call | solution.py:152
  23.2 5.2 %second_sums.1.turned = bf16[3,256,2048]{2,1,0:T(8,128)(2,1)S(1)} custom-call(s32[528]{0:T(1024)S(1)} %copy-done.3, s32[2]{0:T(128)S(1)} %copy-done.4, bf16[1,256,128,128]{3,2,1,0:T(8,128)(2,1)S(1)} %copy-done.2, bf16[16,128,256]{2,1,0:T(8,128)(2,1)} %collective-permute-done.other, f32[49,128,256]{2,1,0:T(8,128)S(1)} %first_sums.1.before), custom_call_target="tpu_custom_call" | custom-call | flops 10000000000 | bytes 16777216 | tf_op jit(solution)/shard_map/second_sums/pallas_call | solution.py:165
  28.5 1.6 %collective-permute-done.2.low = bf16[16,128,256]{2,1,0:T(8,128)(2,1)S(1)} collective-permute-done((bf16[16,128,256]{2,1,0:T(8,128)(2,1)}, bf16[16,128,256]{2,1,0:T(8,128)(2,1)S(1)}, u32[]{:S(2)}, u32[]{:S(2)}) %collective-permute-start.2) | collective-permute-done | bytes 1048608 | tf_op jit(solution)/shard_map/ppermute | solution.py:201
  30.1 2.0 %collective-permute-done.3.high = bf16[16,128,256]{2,1,0:T(8,128)(2,1)S(1)} collective-permute-done((bf16[16,128,256]{2,1,0:T(8,128)(2,1)}, bf16[16,128,256]{2,1,0:T(8,128)(2,1)S(1)}, u32[]{:S(2)}, u32[]{:S(2)}) %collective-permute-start.3) | collective-permute-done | bytes 1048608 | tf_op jit(solution)/shard_map/ppermute | solution.py:201
  32.1 1.2 %couple.1 = f32[2,4,4,8,768]{4,3,2,1,0:T(8,128)S(1)} custom-call(s32[1]{0:T(128)} %bitcast.core, bf16[3,256,2048]{2,1,0:T(8,128)(2,1)S(1)} %second_sums.1.turned, bf16[16,128,256]{2,1,0:T(8,128)(2,1)S(1)} %collective-permute-done.2.low, bf16[16,128,256]{2,1,0:T(8,128)(2,1)S(1)} %copy-done.1, bf16[16,128,256]{2,1,0:T(8,128)(2,1)S(1)} %collective-permute-done.3.high), custom_call_target="tpu_custom_call" | custom-call | flops 1000000000 | bytes 6291456 | tf_op jit(solution)/shard_map/couple/pallas_call | solution.py:189
  33.3 0.9 %collective-permute-start.4 = (f32[4,4,8,768]{3,2,1,0:T(8,128)S(1)}, f32[4,4,8,768]{3,2,1,0:T(8,128)S(1)}, u32[]{:S(2)}, u32[]{:S(2)}) collective-permute-start(f32[4,4,8,768]{3,2,1,0:T(8,128)S(1)} %slice_bitcast_fusion), channel_id=1, source_target_pairs={{0,8},{8,0},{16,24},{24,16},{32,40},{40,32},{48,56},{56,48},{64,72... | collective-permute-start | bytes 1179656 | tf_op jit(solution)/shard_map/ppermute | solution.py:201
  34.3 1.3 %collective-permute-done.4 = f32[4,4,8,768]{3,2,1,0:T(8,128)S(1)} collective-permute-done((f32[4,4,8,768]{3,2,1,0:T(8,128)S(1)}, f32[4,4,8,768]{3,2,1,0:T(8,128)S(1)}, u32[]{:S(2)}, u32[]{:S(2)}) %collective-permute-start.4) | collective-permute-done | bytes 393248 | tf_op jit(solution)/shard_map/ppermute | solution.py:201
  35.7 4.6 %collective-permute-start.7 = (bf16[32,768]{1,0:T(8,128)(2,1)S(1)}, bf16[32,768]{1,0:T(8,128)(2,1)S(1)}, u32[]{:S(2)}, u32[]{:S(2)}) collective-permute-start(bf16[32,768]{1,0:T(8,128)(2,1)S(1)} %get-tuple-element.10), channel_id=1, source_target_pairs={{0,48},{8,56},{16,0},{24,8},{32,16},{40,24},{48,32},{56,40},{64,11... | collective-permute-start | bytes 147464 | tf_op jit(solution)/shard_map/ppermute | solution.py:201
  41.0 0.7 collective-permute-start.5
  42.4 3.6 %collective-permute-done.6 = bf16[32,768]{1,0:T(8,128)(2,1)S(1)} collective-permute-done((bf16[32,768]{1,0:T(8,128)(2,1)S(1)}, bf16[32,768]{1,0:T(8,128)(2,1)S(1)}, u32[]{:S(2)}, u32[]{:S(2)}) %collective-permute-start.6) | collective-permute-done | bytes 49184 | tf_op jit(solution)/shard_map/ppermute | solution.py:201
  46.6 15.2 %collective-permute-start.10 = (f32[8,768]{1,0:T(8,128)S(1)}, f32[8,768]{1,0:T(8,128)S(1)}, u32[]{:S(2)}, u32[]{:S(2)}) collective-permute-start(f32[8,768]{1,0:T(8,128)S(1)} %get-tuple-element.13), channel_id=1, source_target_pairs={{0,192},{8,200},{16,208},{24,216},{32,224},{40,232},{48,240},{56,2... | collective-permute-start | bytes 73736 | tf_op jit(solution)/shard_map/ppermute | solution.py:201
  61.8 1.7 %collective-permute-start.9 = (f32[8,768]{1,0:T(8,128)S(1)}, f32[8,768]{1,0:T(8,128)S(1)}, u32[]{:S(2)}, u32[]{:S(2)}) collective-permute-start(f32[8,768]{1,0:T(8,128)S(1)} %get-tuple-element.14), channel_id=1, source_target_pairs={{0,128},{8,136},{16,144},{24,152},{32,160},{40,168},{48,176},{56,1... | collective-permute-start | bytes 73736 | tf_op jit(solution)/shard_map/ppermute | solution.py:201
  63.5 1.3 %collective-permute-start.8 = (f32[8,768]{1,0:T(8,128)S(1)}, f32[8,768]{1,0:T(8,128)S(1)}, u32[]{:S(2)}, u32[]{:S(2)}) collective-permute-start(f32[8,768]{1,0:T(8,128)S(1)} %get-tuple-element.12), channel_id=1, source_target_pairs={{0,64},{8,72},{16,80},{24,88},{32,96},{40,104},{48,112},{56,120},{... | collective-permute-start | bytes 73736 | tf_op jit(solution)/shard_map/ppermute | solution.py:201
  64.8 2.3 %collective-permute-done.9 = f32[8,768]{1,0:T(8,128)S(1)} collective-permute-done((f32[8,768]{1,0:T(8,128)S(1)}, f32[8,768]{1,0:T(8,128)S(1)}, u32[]{:S(2)}, u32[]{:S(2)}) %collective-permute-start.9) | collective-permute-done | bytes 24608 | tf_op jit(solution)/shard_map/ppermute | solution.py:201
  67.1 1.4 %collective-permute-done.8 = f32[8,768]{1,0:T(8,128)S(1)} collective-permute-done((f32[8,768]{1,0:T(8,128)S(1)}, f32[8,768]{1,0:T(8,128)S(1)}, u32[]{:S(2)}, u32[]{:S(2)}) %collective-permute-start.8) | collective-permute-done | bytes 24608 | tf_op jit(solution)/shard_map/ppermute | solution.py:201
  68.6 2.2 %collective-permute-start.12 = (f32[8,256]{1,0:T(8,128)S(1)}, f32[8,256]{1,0:T(8,128)S(1)}, u32[]{:S(2)}, u32[]{:S(2)}) collective-permute-start(f32[8,256]{1,0:T(8,128)S(1)} %get-tuple-element.16), channel_id=1, source_target_pairs={{1,0},{2,1},{3,2},{4,3},{5,4},{6,5},{7,6},{9,8},{10,9},{11,10},{12... | collective-permute-start | bytes 24584 | tf_op jit(solution)/shard_map/ppermute | solution.py:201
  70.8 3.6 %collective-permute-start.11 = (f32[8,256]{1,0:T(8,128)S(1)}, f32[8,256]{1,0:T(8,128)S(1)}, u32[]{:S(2)}, u32[]{:S(2)}) collective-permute-start(f32[8,256]{1,0:T(8,128)S(1)} %get-tuple-element.15), channel_id=1, source_target_pairs={{0,1},{1,2},{2,3},{3,4},{4,5},{5,6},{6,7},{8,9},{9,10},{10,11},{11... | collective-permute-start | bytes 24584 | tf_op jit(solution)/shard_map/ppermute | solution.py:201
  74.4 3.1 %collective-permute-done.11 = f32[8,256]{1,0:T(8,128)S(1)} collective-permute-done((f32[8,256]{1,0:T(8,128)S(1)}, f32[8,256]{1,0:T(8,128)S(1)}, u32[]{:S(2)}, u32[]{:S(2)}) %collective-permute-start.11) | collective-permute-done | bytes 8224 | tf_op jit(solution)/shard_map/ppermute | solution.py:201
  (24 shorter events, 4.0 us)
Async XLA Ops:
  0.0 11.6 %collective-permute-start.1 = (bf16[16,128,256]{2,1,0:T(8,128)(2,1)}, bf16[16,128,256]{2,1,0:T(8,128)(2,1)}, u32[]{:S(2)}, u32[]{:S(2)}) collective-permute-start(bf16[16,128,256]{2,1,0:T(8,128)(2,1)} %own.3), channel_id=1, source_target_pairs={{0,8},{8,0},{16,24},{24,16},{32,40},{40,32},{48,56},{56,48},{64,72... | collective-permute-start | bytes 3145736 | tf_op jit(solution)/shard_map/ppermute | solution.py:201
  0.0 23.2 %collective-permute-start = (bf16[16,128,256]{2,1,0:T(8,128)(2,1)}, bf16[16,128,256]{2,1,0:T(8,128)(2,1)}, u32[]{:S(2)}, u32[]{:S(2)}) collective-permute-start(bf16[16,128,256]{2,1,0:T(8,128)(2,1)} %own.3), channel_id=1, source_target_pairs={{8,16},{24,32},{40,48},{56,64},{72,80},{88,96},{104,112},{120,128}... | collective-permute-start | bytes 3145736 | tf_op jit(solution)/shard_map/ppermute | solution.py:201
  1.6 28.4 %collective-permute-start.2 = (bf16[16,128,256]{2,1,0:T(8,128)(2,1)}, bf16[16,128,256]{2,1,0:T(8,128)(2,1)S(1)}, u32[]{:S(2)}, u32[]{:S(2)}) collective-permute-start(bf16[16,128,256]{2,1,0:T(8,128)(2,1)} %own.3), channel_id=1, source_target_pairs={{0,1},{1,2},{2,3},{3,4},{4,5},{5,6},{6,7},{8,9},{9,10},{10,11},{11... | collective-permute-start | bytes 3145736 | tf_op jit(solution)/shard_map/ppermute | solution.py:201
  4.6 27.6 %collective-permute-start.3 = (bf16[16,128,256]{2,1,0:T(8,128)(2,1)}, bf16[16,128,256]{2,1,0:T(8,128)(2,1)S(1)}, u32[]{:S(2)}, u32[]{:S(2)}) collective-permute-start(bf16[16,128,256]{2,1,0:T(8,128)(2,1)} %own.3), channel_id=1, source_target_pairs={{1,0},{2,1},{3,2},{4,3},{5,4},{6,5},{7,6},{9,8},{10,9},{11,10},{12... | collective-permute-start | bytes 3145736 | tf_op jit(solution)/shard_map/ppermute | solution.py:201
  11.6 1.2 %copy-start = (bf16[16,128,256]{2,1,0:T(8,128)(2,1)S(1)}, bf16[16,128,256]{2,1,0:T(8,128)(2,1)}, u32[]{:S(2)}) copy-start(bf16[16,128,256]{2,1,0:T(8,128)(2,1)} %own.3) | copy-start | bytes 3145732
  12.8 3.4 %copy-start.2 = (bf16[1,256,128,128]{3,2,1,0:T(8,128)(2,1)S(1)}, bf16[1,256,128,128]{3,2,1,0:T(8,128)(2,1)}, u32[]{:S(2)}) copy-start(bf16[1,256,128,128]{3,2,1,0:T(8,128)(2,1)} %a_hbm.3) | copy-start | bytes 25165828
  16.2 0.7 copy-start.3
  16.9 0.6 copy-start.4
  23.2 8.9 %copy-start.1 = (bf16[16,128,256]{2,1,0:T(8,128)(2,1)S(1)}, bf16[16,128,256]{2,1,0:T(8,128)(2,1)}, u32[]{:S(2)}) copy-start(bf16[16,128,256]{2,1,0:T(8,128)(2,1)} %own.3) | copy-start | bytes 3145732
  33.3 2.3 %collective-permute-start.4 = (f32[4,4,8,768]{3,2,1,0:T(8,128)S(1)}, f32[4,4,8,768]{3,2,1,0:T(8,128)S(1)}, u32[]{:S(2)}, u32[]{:S(2)}) collective-permute-start(f32[4,4,8,768]{3,2,1,0:T(8,128)S(1)} %slice_bitcast_fusion), channel_id=1, source_target_pairs={{0,8},{8,0},{16,24},{24,16},{32,40},{40,32},{48,56},{56,48},{64,72... | collective-permute-start | bytes 1179656 | tf_op jit(solution)/shard_map/ppermute | solution.py:201
  35.7 6.7 %collective-permute-start.7 = (bf16[32,768]{1,0:T(8,128)(2,1)S(1)}, bf16[32,768]{1,0:T(8,128)(2,1)S(1)}, u32[]{:S(2)}, u32[]{:S(2)}) collective-permute-start(bf16[32,768]{1,0:T(8,128)(2,1)S(1)} %get-tuple-element.10), channel_id=1, source_target_pairs={{0,48},{8,56},{16,0},{24,8},{32,16},{40,24},{48,32},{56,40},{64,11... | collective-permute-start | bytes 147464 | tf_op jit(solution)/shard_map/ppermute | solution.py:201
  40.3 5.8 %collective-permute-start.6 = (bf16[32,768]{1,0:T(8,128)(2,1)S(1)}, bf16[32,768]{1,0:T(8,128)(2,1)S(1)}, u32[]{:S(2)}, u32[]{:S(2)}) collective-permute-start(bf16[32,768]{1,0:T(8,128)(2,1)S(1)} %get-tuple-element.11), channel_id=1, source_target_pairs={{0,32},{8,40},{16,48},{24,56},{32,0},{40,8},{48,16},{56,24},{64,96... | collective-permute-start | bytes 147464 | tf_op jit(solution)/shard_map/ppermute | solution.py:201
  41.0 5.6 %collective-permute-start.5 = (bf16[32,768]{1,0:T(8,128)(2,1)S(1)}, bf16[32,768]{1,0:T(8,128)(2,1)S(1)}, u32[]{:S(2)}, u32[]{:S(2)}) collective-permute-start(bf16[32,768]{1,0:T(8,128)(2,1)S(1)} %get-tuple-element.9), channel_id=1, source_target_pairs={{0,16},{8,24},{16,32},{24,40},{32,48},{40,56},{48,0},{56,8},{64,80... | collective-permute-start | bytes 147464 | tf_op jit(solution)/shard_map/ppermute | solution.py:201
  46.6 18.2 %collective-permute-start.10 = (f32[8,768]{1,0:T(8,128)S(1)}, f32[8,768]{1,0:T(8,128)S(1)}, u32[]{:S(2)}, u32[]{:S(2)}) collective-permute-start(f32[8,768]{1,0:T(8,128)S(1)} %get-tuple-element.13), channel_id=1, source_target_pairs={{0,192},{8,200},{16,208},{24,216},{32,224},{40,232},{48,240},{56,2... | collective-permute-start | bytes 73736 | tf_op jit(solution)/shard_map/ppermute | solution.py:201
  61.8 5.3 %collective-permute-start.9 = (f32[8,768]{1,0:T(8,128)S(1)}, f32[8,768]{1,0:T(8,128)S(1)}, u32[]{:S(2)}, u32[]{:S(2)}) collective-permute-start(f32[8,768]{1,0:T(8,128)S(1)} %get-tuple-element.14), channel_id=1, source_target_pairs={{0,128},{8,136},{16,144},{24,152},{32,160},{40,168},{48,176},{56,1... | collective-permute-start | bytes 73736 | tf_op jit(solution)/shard_map/ppermute | solution.py:201
  63.5 5.0 %collective-permute-start.8 = (f32[8,768]{1,0:T(8,128)S(1)}, f32[8,768]{1,0:T(8,128)S(1)}, u32[]{:S(2)}, u32[]{:S(2)}) collective-permute-start(f32[8,768]{1,0:T(8,128)S(1)} %get-tuple-element.12), channel_id=1, source_target_pairs={{0,64},{8,72},{16,80},{24,88},{32,96},{40,104},{48,112},{56,120},{... | collective-permute-start | bytes 73736 | tf_op jit(solution)/shard_map/ppermute | solution.py:201
  68.6 5.9 %collective-permute-start.12 = (f32[8,256]{1,0:T(8,128)S(1)}, f32[8,256]{1,0:T(8,128)S(1)}, u32[]{:S(2)}, u32[]{:S(2)}) collective-permute-start(f32[8,256]{1,0:T(8,128)S(1)} %get-tuple-element.16), channel_id=1, source_target_pairs={{1,0},{2,1},{3,2},{4,3},{5,4},{6,5},{7,6},{9,8},{10,9},{11,10},{12... | collective-permute-start | bytes 24584 | tf_op jit(solution)/shard_map/ppermute | solution.py:201
  70.8 6.8 %collective-permute-start.11 = (f32[8,256]{1,0:T(8,128)S(1)}, f32[8,256]{1,0:T(8,128)S(1)}, u32[]{:S(2)}, u32[]{:S(2)}) collective-permute-start(f32[8,256]{1,0:T(8,128)S(1)} %get-tuple-element.15), channel_id=1, source_target_pairs={{0,1},{1,2},{2,3},{3,4},{4,5},{5,6},{6,7},{8,9},{9,10},{10,11},{11... | collective-permute-start | bytes 24584 | tf_op jit(solution)/shard_map/ppermute | solution.py:201

commit v2 on v0

v2 whole, which is shorter than its diff:
```python
import functools

import jax
import jax.numpy as jnp
from jax import lax
from jax.experimental import pallas as pl
from jax.experimental.pallas import tpu as pltpu
from jax.sharding import PartitionSpec as P

BF = jnp.bfloat16
F32 = jnp.float32
PANELS = 16
TILE = 128
BAND = 256
SLOTS = 256
UNROLL = 16
STEP = 8
LIST = SLOTS + UNROLL
SM = pl.BlockSpec(memory_space=pltpu.SMEM)
VM = pl.BlockSpec(memory_space=pltpu.VMEM)
SUMS = (3 * PANELS + 1, TILE, BAND)
X, Y = 4, 4
TERMS = (2, X, Y, 3, 8, BAND)


def vmem(mib):
    return pltpu.CompilerParams(vmem_limit_bytes=mib * 2**20)


def cost(flops, nbytes):
    return pl.CostEstimate(flops=flops, bytes_accessed=nbytes, transcendentals=0)


def plan_kernel(rows, cols, count, codes, counts):
    live = count[0, 0]

    def put(step, pos):
        n = list(pos)
        for u in range(STEP):
            t = step * STEP + u
            r, c = rows[0, t], cols[0, t]
            q = c >> 4
            base = jnp.where(q == 0, n[0], jnp.where(q == 1, n[1], n[2]))
            ok = t < live
            codes[jnp.where(ok, base, 3 * LIST)] = t * 1024 + r * 16 + (c & 15)
            n = [n[i] + (ok & (q == i)).astype(jnp.int32) for i in range(3)]
        return tuple(n)

    steps = (live + STEP - 1) // STEP
    ends = lax.fori_loop(0, steps, put, tuple(jnp.int32(i * LIST) for i in range(3)))
    for i in range(3):
        counts[i] = ends[i] - i * LIST
        for u in range(UNROLL):
            codes[ends[i] + u] = 3 * PANELS * 16


def plan(rows, cols, count):
    return pl.pallas_call(
        plan_kernel,
        out_shape=(
            jax.ShapeDtypeStruct((3 * LIST + 1,), jnp.int32),
            jax.ShapeDtypeStruct((3,), jnp.int32),
        ),
        in_specs=[SM] * 3,
        out_specs=(SM, SM),
        compiler_params=vmem(2),
        name="plan",
        cost_estimate=cost(30 * 10**9, 10**4),
    )(rows, cols, count)


def apply_tiles(which, codes, counts, a_tiles, panels, sums):
    def step(g, carry):
        applied, rows = [], []
        for u in range(UNROLL):
            code = codes[which * LIST + g * UNROLL + u]
            rows.append((code >> 4) & 63)
            product = jnp.dot(a_tiles[0, code >> 10], panels[code & 15], preferred_element_type=F32)
            applied.append(product.astype(BF).astype(F32))
        for u in range(UNROLL):
            sums[rows[u]] += applied[u]
        return carry

    lax.fori_loop(0, (counts[which] + UNROLL - 1) // UNROLL, step, 0)


def first_kernel(place, codes, counts, a_tiles, own, partner, sums):
    def zero(i, carry):
        sums[i] = jnp.zeros((TILE, BAND), F32)
        return carry

    lax.fori_loop(0, 3 * PANELS + 1, zero, 0)
    apply_tiles(1, codes, counts, a_tiles, own, sums)
    apply_tiles(2 - 2 * (place[0] & 1), codes, counts, a_tiles, partner, sums)


def put_term(row, turned, panels, slot, terms):
    term = jnp.dot(turned, panels[...].reshape(PANELS * TILE, BAND), preferred_element_type=F32).T
    for block in range(BAND // 8):
        to = row ^ block
        terms[to & 1, (to >> 1) & 3, to >> 3, slot] = term[block * 8:(block + 1) * 8]


def second_kernel(place, codes, counts, a_tiles, other, before, own, sums, turned, terms):
    apply_tiles(2 * (place[0] & 1), codes, counts, a_tiles, other, sums)
    for k in range(3 * PANELS):
        lanes = pl.ds((k % PANELS) * TILE, TILE)
        turned[k // PANELS, :, lanes] = sums[k].astype(BF).T
    put_term(place[0], turned[1], own, 1, terms)


def first_sums(place, codes, counts, a_tiles, own, partner):
    return pl.pallas_call(
        first_kernel,
        out_shape=jax.ShapeDtypeStruct(SUMS, F32),
        in_specs=[SM] * 3 + [VM] * 3,
        out_specs=VM,
        compiler_params=vmem(20),
        name="first_sums",
        cost_estimate=cost(10 * 10**9, 16 * 2**20),
    )(place, codes, counts, a_tiles, own, partner)


def second_sums(place, codes, counts, a_tiles, other, before, own):
    return pl.pallas_call(
        second_kernel,
        out_shape=(
            jax.ShapeDtypeStruct(SUMS, F32),
            jax.ShapeDtypeStruct((3, BAND, PANELS * TILE), BF),
            jax.ShapeDtypeStruct(TERMS, F32),
        ),
        in_specs=[SM] * 3 + [VM] * 4,
        out_specs=(VM, VM, VM),
        input_output_aliases={5: 0},
        compiler_params=vmem(24),
        name="second_sums",
        cost_estimate=cost(10 * 10**9, 16 * 2**20),
    )(place, codes, counts, a_tiles, other, before, own)[1:]


def couple_kernel(place, turned, even, odd, before, terms):
    even_offset = place[1]
    put_term(place[0], turned[even_offset], even, 0, terms)
    put_term(place[0], turned[2 - even_offset], odd, 2, terms)


def couple(place, turned, even, odd, before):
    return pl.pallas_call(
        couple_kernel,
        out_shape=jax.ShapeDtypeStruct(TERMS, F32),
        in_specs=[SM] + [VM] * 4,
        out_specs=VM,
        input_output_aliases={4: 0},
        compiler_params=vmem(12),
        name="couple",
        cost_estimate=cost(10**9, 6 * 2**20),
    )(place, turned, even, odd, before)


def swap_sum(value, shift, kind):
    total = value[0]
    for i in range(1, value.shape[0]):
        pairs = [(r, r ^ (i << shift)) for r in range(2 * X * Y)]
        total = total + lax.ppermute(value[i].astype(kind), "row", pairs).astype(F32)
    return total


def both_ways(pairs):
    return pairs + [(j, i) for i, j in pairs]


def local(a_tiles, a_rows, a_cols, a_count, p_panels):
    n_row, n_col = lax.axis_size("row"), lax.axis_size("col")
    row, col = lax.axis_index("row"), lax.axis_index("col")
    even_pairs = both_ways([(i, i + 1) for i in range(0, n_col - 1, 2)])
    odd_pairs = both_ways([(i, i + 1) for i in range(1, n_col - 1, 2)])
    chip = both_ways([(i, i + 1) for i in range(0, n_row - 1, 2)])
    bridges = both_ways([(i, i + 1) for i in range(1, n_row - 1, 2)])
    even = lax.ppermute(p_panels, "col", even_pairs)
    odd = lax.ppermute(p_panels, "col", odd_pairs)
    other = lax.ppermute(p_panels, "row", bridges)
    partner = lax.ppermute(p_panels, "row", chip)
    low_col = (col & 1) == 0
    place = jnp.stack([row, jnp.where(low_col, 2, 0)]).astype(jnp.int32)
    codes, counts = plan(a_rows, a_cols, a_count)
    before = first_sums(place, codes, counts, a_tiles, p_panels, partner)
    turned, terms = second_sums(place, codes, counts, a_tiles, other, before, p_panels)
    terms = couple(place, turned, even, odd, terms)
    terms = swap_sum(terms, 0, F32)
    terms = swap_sum(terms, 1, BF)
    terms = swap_sum(terms, 3, F32)
    from_even = lax.ppermute(terms[0], "col", even_pairs)
    from_odd = lax.ppermute(terms[2], "col", odd_pairs)
    lower = jnp.where(low_col, from_odd, from_even)
    upper = jnp.where(low_col, from_even, from_odd)
    return jnp.concatenate([lower, terms[1], upper], axis=1)[None]


def solution(mesh):
    in_specs = (
        P("row", "col", None, None),
        P("row", "col"),
        P("row", "col"),
        P("row", "col"),
        P(("row", "col"), None, None),
    )
    out_specs = P("col", "row", None)
    return jax.shard_map(local, mesh=mesh, in_specs=in_specs, out_specs=out_specs, check_vma=False)
```

time: 421 us -> 63.7 us (0.15)
  the two profiles are of different devices: /device:TPU:1 before, /device:TPU:96 now
where the time goes in v2:
time: 63.7 us; the launch traced here: 63.4 us
  starting transfers between devices  24.2 us (38%)
  waiting for transfers between devices  20.8 us (33%)
  Pallas kernels  12 us (19%)
  local copies, waits for them, and re-layouts  4.79 us (8%)
  between operations  0.79 us (1%)
  other arithmetic  0.78 us (1%)
    ppermute x7, starting transfers between devices, swap_sum(): lax.ppermute(value[i].astype(kind), 'row', pairs).astype(F32)  11.6 us
    ppermute x7, waiting for transfers between devices, swap_sum(): lax.ppermute(value[i].astype(kind), 'row', pairs).astype(F32)  10.1 us
    ppermute x1, starting transfers between devices, local(): odd = lax.ppermute(p_panels, 'col', odd_pairs)  5.93 us
    ppermute x1, starting transfers between devices, local(): from_odd = lax.ppermute(terms[2], 'col', odd_pairs)  4.86 us
    unnamed x10, local copies, waits for them, and re-layouts  4.74 us
    pallas_call x1, Pallas kernels, first_sums(): pl.pallas_call(first_kernel, out_shape=jax.ShapeDtypeStruct(SUMS, F32), i...  4.63 us
    ppermute x1, waiting for transfers between devices, local(): odd = lax.ppermute(p_panels, 'col', odd_pairs)  4.01 us
    pallas_call x1, Pallas kernels, second_sums(): pl.pallas_call(second_kernel, out_shape=(jax.ShapeDtypeStruct(SUMS, F32),...  3.7 us
  transfers between devices with their start and end apart: 13, of which 10 were waited for; matrix products, arithmetic and copies ran while one was open for 0% of the time, Pallas kernels for 17%

profile of v2, /device:TPU:96, one launch (start us, length us, event | category | flops | bytes accessed | tf_op | source)
XLA Modules:
  0.0 63.4 jit_solution(3184872834572313063)
XLA Ops:
  0.0 1.6 %collective-permute-start = (bf16[16,128,256]{2,1,0:T(8,128)(2,1)}, bf16[16,128,256]{2,1,0:T(8,128)(2,1)}, u32[]{:S(2)}, u32[]{:S(2)}) collective-permute-start(bf16[16,128,256]{2,1,0:T(8,128)(2,1)} %own.3), channel_id=1, source_target_pairs={{8,16},{24,32},{40,48},{56,64},{72,80},{88,96},{104,112},{120,128}... | collective-permute-start | bytes 3145736 | tf_op jit(solution)/shard_map/ppermute | solution.py:181
  1.8 5.9 %collective-permute-start.3 = (bf16[16,128,256]{2,1,0:T(8,128)(2,1)}, bf16[16,128,256]{2,1,0:T(8,128)(2,1)S(1)}, u32[]{:S(2)}, u32[]{:S(2)}) collective-permute-start(bf16[16,128,256]{2,1,0:T(8,128)(2,1)} %own.3), channel_id=1, source_target_pairs={{1,2},{3,4},{5,6},{2,1},{4,3},{6,5},{9,10},{11,12},{13,14},{10,9},... | collective-permute-start | bytes 3145736 | tf_op jit(solution)/shard_map/ppermute | solution.py:180
  8.4 0.7 %copy-done.3 = s32[1,256]{1,0:T(1,128)S(1)} copy-done((s32[1,256]{1,0:T(1,128)S(1)}, s32[1,256]{1,0:T(1,128)}, u32[]{:S(2)}) %copy-start.3) | copy-done | bytes 1048
  9.0 0.7 %copy-done.4 = s32[1,256]{1,0:T(1,128)S(1)} copy-done((s32[1,256]{1,0:T(1,128)S(1)}, s32[1,256]{1,0:T(1,128)}, u32[]{:S(2)}) %copy-start.4) | copy-done | bytes 1048
  9.7 2.3 %plan.1 = (s32[817]{0:T(1024)S(1)}, s32[3]{0:T(128)S(1)}) custom-call(s32[1,256]{1,0:T(1,128)S(1)} %copy-done.3, s32[1,256]{1,0:T(1,128)S(1)} %copy-done.4, s32[1,1]{1,0:T(1,128)S(6)} %copy.10.count), custom_call_target="tpu_custom_call" | custom-call | flops 30000001024 | bytes 10000 | tf_op jit(solution)/shard_map/plan/pallas_call | solution.py:58
  12.1 3.4 %copy-done = bf16[1,256,128,128]{3,2,1,0:T(8,128)(2,1)S(1)} copy-done((bf16[1,256,128,128]{3,2,1,0:T(8,128)(2,1)S(1)}, bf16[1,256,128,128]{3,2,1,0:T(8,128)(2,1)}, u32[]{:S(2)}) %copy-start) | copy-done | bytes 8388632
  15.5 4.6 %first_sums.1.before = f32[49,128,256]{2,1,0:T(8,128)S(1)} custom-call(s32[2]{0:T(128)S(1)} %pad_add_fusion.place, s32[817]{0:T(1024)S(1)} %get-tuple-element.9.codes, s32[3]{0:T(128)S(1)} %get-tuple-element.10.counts, bf16[1,256,128,128]{3,2,1,0:T(8,128)(2,1)S(1)} %copy-done, bf16[16,128,256]{2,1,0:T(8,128)(2,1)S(1)} %copy-done.2, ...), custom_call_target="tpu_custom_call" | custom-call | flops 10000000000 | bytes 16777216 | tf_op jit(solution)/shard_map/first_sums/pallas_call | solution.py:113
  20.1 3.7 %second_sums.1 = (f32[49,128,256]{2,1,0:T(8,128)S(1)}, bf16[3,256,2048]{2,1,0:T(8,128)(2,1)S(1)}, f32[2,4,4,3,8,256]{5,4,3,2,1,0:T(8,128)S(1)}) custom-call(s32[2]{0:T(128)S(1)} %pad_add_fusion.place, s32[817]{0:T(1024)S(1)} %get-tuple-element.9.codes, s32[3]{0:T(128)S(1)} %get-tuple-element.10.counts, ...), custom_call_target="tpu_custom_call", output_to_operand_aliasing={{0}: (5, {})} | custom-call | flops 10000000000 | bytes 16777216 | tf_op jit(solution)/shard_map/second_sums/pallas_call | solution.py:125
  23.8 3.1 %collective-permute-done.2.even = bf16[16,128,256]{2,1,0:T(8,128)(2,1)S(1)} collective-permute-done((bf16[16,128,256]{2,1,0:T(8,128)(2,1)}, bf16[16,128,256]{2,1,0:T(8,128)(2,1)S(1)}, u32[]{:S(2)}, u32[]{:S(2)}) %collective-permute-start.2) | collective-permute-done | bytes 1048608 | tf_op jit(solution)/shard_map/ppermute | solution.py:179
  26.9 4.0 %collective-permute-done.3.odd = bf16[16,128,256]{2,1,0:T(8,128)(2,1)S(1)} collective-permute-done((bf16[16,128,256]{2,1,0:T(8,128)(2,1)}, bf16[16,128,256]{2,1,0:T(8,128)(2,1)S(1)}, u32[]{:S(2)}, u32[]{:S(2)}) %collective-permute-start.3) | collective-permute-done | bytes 1048608 | tf_op jit(solution)/shard_map/ppermute | solution.py:180
  30.9 1.4 %couple.1 = f32[2,4,4,3,8,256]{5,4,3,2,1,0:T(8,128)S(1)} custom-call(s32[2]{0:T(128)S(1)} %pad_add_fusion.place, bf16[3,256,2048]{2,1,0:T(8,128)(2,1)S(1)} %get-tuple-element.11.turned, bf16[16,128,256]{2,1,0:T(8,128)(2,1)S(1)} %collective-permute-done.2.even, bf16[16,128,256]{2,1,0:T(8,128)(2,1)S(1)} %collective-permute-done.3.odd, ...), custom_call_target="tpu_custom_call", output_to_operand_aliasing={{}: (4, {})} | custom-call | flops 1000000000 | bytes 6291456 | tf_op jit(solution)/shard_map/couple/pallas_call | solution.py:148
  32.4 0.9 %collective-permute-start.4 = (f32[4,4,3,8,256]{4,3,2,1,0:T(8,128)S(1)}, f32[4,4,3,8,256]{4,3,2,1,0:T(8,128)S(1)}, u32[]{:S(2)}, u32[]{:S(2)}) collective-permute-start(f32[4,4,3,8,256]{4,3,2,1,0:T(8,128)S(1)} %slice_bitcast_fusion), channel_id=1, source_target_pairs={{0,8},{8,0},{16,24},{24,16},{32,40},{40,32},{48,56},{56,48},{64,72... | collective-permute-start | bytes 1179656 | tf_op jit(solution)/shard_map/ppermute | solution.py:164
  33.3 1.3 %collective-permute-done.4 = f32[4,4,3,8,256]{4,3,2,1,0:T(8,128)S(1)} collective-permute-done((f32[4,4,3,8,256]{4,3,2,1,0:T(8,128)S(1)}, f32[4,4,3,8,256]{4,3,2,1,0:T(8,128)S(1)}, u32[]{:S(2)}, u32[]{:S(2)}) %collective-permute-start.4) | collective-permute-done | bytes 393248 | tf_op jit(solution)/shard_map/ppermute | solution.py:164
  34.7 3.1 %collective-permute-start.5 = (bf16[4,3,8,256]{3,2,1,0:T(8,128)(2,1)S(1)}, bf16[4,3,8,256]{3,2,1,0:T(8,128)(2,1)S(1)}, u32[]{:S(2)}, u32[]{:S(2)}) collective-permute-start(bf16[4,3,8,256]{3,2,1,0:T(8,128)(2,1)S(1)} %get-tuple-element.15), channel_id=1, source_target_pairs={{0,16},{8,24},{16,0},{24,8},{32,48},{40,56},{48,32},{56,40},{64,80... | collective-permute-start | bytes 147464 | tf_op jit(solution)/shard_map/ppermute | solution.py:164
  37.8 2.7 %collective-permute-start.6 = (bf16[4,3,8,256]{3,2,1,0:T(8,128)(2,1)S(1)}, bf16[4,3,8,256]{3,2,1,0:T(8,128)(2,1)S(1)}, u32[]{:S(2)}, u32[]{:S(2)}) collective-permute-start(bf16[4,3,8,256]{3,2,1,0:T(8,128)(2,1)S(1)} %get-tuple-element.17), channel_id=1, source_target_pairs={{0,32},{8,40},{16,48},{24,56},{32,0},{40,8},{48,16},{56,24},{64,96... | collective-permute-start | bytes 147464 | tf_op jit(solution)/shard_map/ppermute | solution.py:164
  40.6 2.8 %collective-permute-done.6 = bf16[4,3,8,256]{3,2,1,0:T(8,128)(2,1)S(1)} collective-permute-done((bf16[4,3,8,256]{3,2,1,0:T(8,128)(2,1)S(1)}, bf16[4,3,8,256]{3,2,1,0:T(8,128)(2,1)S(1)}, u32[]{:S(2)}, u32[]{:S(2)}) %collective-permute-start.6) | collective-permute-done | bytes 49184 | tf_op jit(solution)/shard_map/ppermute | solution.py:164
  43.4 2.4 %collective-permute-done.7 = bf16[4,3,8,256]{3,2,1,0:T(8,128)(2,1)S(1)} collective-permute-done((bf16[4,3,8,256]{3,2,1,0:T(8,128)(2,1)S(1)}, bf16[4,3,8,256]{3,2,1,0:T(8,128)(2,1)S(1)}, u32[]{:S(2)}, u32[]{:S(2)}) %collective-permute-start.7) | collective-permute-done | bytes 49184 | tf_op jit(solution)/shard_map/ppermute | solution.py:164
  45.9 1.7 %collective-permute-start.10 = (f32[3,8,256]{2,1,0:T(8,128)S(1)}, f32[3,8,256]{2,1,0:T(8,128)S(1)}, u32[]{:S(2)}, u32[]{:S(2)}) collective-permute-start(f32[3,8,256]{2,1,0:T(8,128)S(1)} %get-tuple-element.19), channel_id=1, source_target_pairs={{0,192},{8,200},{16,208},{24,216},{32,224},{40,232},{48,240},{56,2... | collective-permute-start | bytes 73736 | tf_op jit(solution)/shard_map/ppermute | solution.py:164
  47.6 1.2 %collective-permute-start.8 = (f32[3,8,256]{2,1,0:T(8,128)S(1)}, f32[3,8,256]{2,1,0:T(8,128)S(1)}, u32[]{:S(2)}, u32[]{:S(2)}) collective-permute-start(f32[3,8,256]{2,1,0:T(8,128)S(1)} %get-tuple-element.18), channel_id=1, source_target_pairs={{0,64},{8,72},{16,80},{24,88},{32,96},{40,104},{48,112},{56,120},{... | collective-permute-start | bytes 73736 | tf_op jit(solution)/shard_map/ppermute | solution.py:164
  48.8 1.8 %collective-permute-start.9 = (f32[3,8,256]{2,1,0:T(8,128)S(1)}, f32[3,8,256]{2,1,0:T(8,128)S(1)}, u32[]{:S(2)}, u32[]{:S(2)}) collective-permute-start(f32[3,8,256]{2,1,0:T(8,128)S(1)} %get-tuple-element.20), channel_id=1, source_target_pairs={{0,128},{8,136},{16,144},{24,152},{32,160},{40,168},{48,176},{56,1... | collective-permute-start | bytes 73736 | tf_op jit(solution)/shard_map/ppermute | solution.py:164
  51.4 2.7 %collective-permute-done.9 = f32[3,8,256]{2,1,0:T(8,128)S(1)} collective-permute-done((f32[3,8,256]{2,1,0:T(8,128)S(1)}, f32[3,8,256]{2,1,0:T(8,128)S(1)}, u32[]{:S(2)}, u32[]{:S(2)}) %collective-permute-start.9) | collective-permute-done | bytes 24608 | tf_op jit(solution)/shard_map/ppermute | solution.py:164
  54.2 4.9 %collective-permute-start.11 = (f32[8,256]{1,0:T(8,128)S(1)}, f32[8,256]{1,0:T(8,128)S(1)}, u32[]{:S(2)}, u32[]{:S(2)}) collective-permute-start(f32[8,256]{1,0:T(8,128)S(1)} %get-tuple-element.23), channel_id=1, source_target_pairs={{1,2},{3,4},{5,6},{2,1},{4,3},{6,5},{9,10},{11,12},{13,14},{10,9},... | collective-permute-start | bytes 24584 | tf_op jit(solution)/shard_map/ppermute | solution.py:193
  59.2 1.8 %collective-permute-done.11 = f32[8,256]{1,0:T(8,128)S(1)} collective-permute-done((f32[8,256]{1,0:T(8,128)S(1)}, f32[8,256]{1,0:T(8,128)S(1)}, u32[]{:S(2)}, u32[]{:S(2)}) %collective-permute-start.11) | collective-permute-done | bytes 8224 | tf_op jit(solution)/shard_map/ppermute | solution.py:193
  60.9 1.8 %collective-permute-done.12 = f32[8,256]{1,0:T(8,128)S(1)} collective-permute-done((f32[8,256]{1,0:T(8,128)S(1)}, f32[8,256]{1,0:T(8,128)S(1)}, u32[]{:S(2)}, u32[]{:S(2)}) %collective-permute-start.12) | collective-permute-done | bytes 8224 | tf_op jit(solution)/shard_map/ppermute | solution.py:192
  (26 shorter events, 1.8 us)
Async XLA Ops:
  0.0 12.1 %collective-permute-start.1 = (bf16[16,128,256]{2,1,0:T(8,128)(2,1)}, bf16[16,128,256]{2,1,0:T(8,128)(2,1)}, u32[]{:S(2)}, u32[]{:S(2)}) collective-permute-start(bf16[16,128,256]{2,1,0:T(8,128)(2,1)} %own.3), channel_id=1, source_target_pairs={{0,8},{16,24},{32,40},{48,56},{64,72},{80,88},{96,104},{112,120},{... | collective-permute-start | bytes 3145736 | tf_op jit(solution)/shard_map/ppermute | solution.py:182
  0.0 20.1 %collective-permute-start = (bf16[16,128,256]{2,1,0:T(8,128)(2,1)}, bf16[16,128,256]{2,1,0:T(8,128)(2,1)}, u32[]{:S(2)}, u32[]{:S(2)}) collective-permute-start(bf16[16,128,256]{2,1,0:T(8,128)(2,1)} %own.3), channel_id=1, source_target_pairs={{8,16},{24,32},{40,48},{56,64},{72,80},{88,96},{104,112},{120,128}... | collective-permute-start | bytes 3145736 | tf_op jit(solution)/shard_map/ppermute | solution.py:181
  1.7 25.3 %collective-permute-start.2 = (bf16[16,128,256]{2,1,0:T(8,128)(2,1)}, bf16[16,128,256]{2,1,0:T(8,128)(2,1)S(1)}, u32[]{:S(2)}, u32[]{:S(2)}) collective-permute-start(bf16[16,128,256]{2,1,0:T(8,128)(2,1)} %own.3), channel_id=1, source_target_pairs={{0,1},{2,3},{4,5},{6,7},{1,0},{3,2},{5,4},{7,6},{8,9},{10,11},{12,... | collective-permute-start | bytes 3145736 | tf_op jit(solution)/shard_map/ppermute | solution.py:179
  1.8 29.2 %collective-permute-start.3 = (bf16[16,128,256]{2,1,0:T(8,128)(2,1)}, bf16[16,128,256]{2,1,0:T(8,128)(2,1)S(1)}, u32[]{:S(2)}, u32[]{:S(2)}) collective-permute-start(bf16[16,128,256]{2,1,0:T(8,128)(2,1)} %own.3), channel_id=1, source_target_pairs={{1,2},{3,4},{5,6},{2,1},{4,3},{6,5},{9,10},{11,12},{13,14},{10,9},... | collective-permute-start | bytes 3145736 | tf_op jit(solution)/shard_map/ppermute | solution.py:180
  8.3 0.7 %copy-start.3 = (s32[1,256]{1,0:T(1,128)S(1)}, s32[1,256]{1,0:T(1,128)}, u32[]{:S(2)}) copy-start(s32[1,256]{1,0:T(1,128)} %rows.1) | copy-start | bytes 3076
  9.0 0.7 %copy-start.4 = (s32[1,256]{1,0:T(1,128)S(1)}, s32[1,256]{1,0:T(1,128)}, u32[]{:S(2)}) copy-start(s32[1,256]{1,0:T(1,128)} %cols.1) | copy-start | bytes 3076
  9.7 2.4 %copy-start.2 = (bf16[16,128,256]{2,1,0:T(8,128)(2,1)S(1)}, bf16[16,128,256]{2,1,0:T(8,128)(2,1)}, u32[]{:S(2)}) copy-start(bf16[16,128,256]{2,1,0:T(8,128)(2,1)} %own.3) | copy-start | bytes 3145732
  12.1 3.4 %copy-start = (bf16[1,256,128,128]{3,2,1,0:T(8,128)(2,1)S(1)}, bf16[1,256,128,128]{3,2,1,0:T(8,128)(2,1)}, u32[]{:S(2)}) copy-start(bf16[1,256,128,128]{3,2,1,0:T(8,128)(2,1)} %a_tiles.3) | copy-start | bytes 25165828
  15.5 4.7 %copy-start.1 = (bf16[1,256,128,128]{3,2,1,0:T(8,128)(2,1)S(1)}, bf16[1,256,128,128]{3,2,1,0:T(8,128)(2,1)}, u32[]{:S(2)}) copy-start(bf16[1,256,128,128]{3,2,1,0:T(8,128)(2,1)} %a_tiles.3) | copy-start | bytes 25165828
  32.4 2.2 %collective-permute-start.4 = (f32[4,4,3,8,256]{4,3,2,1,0:T(8,128)S(1)}, f32[4,4,3,8,256]{4,3,2,1,0:T(8,128)S(1)}, u32[]{:S(2)}, u32[]{:S(2)}) collective-permute-start(f32[4,4,3,8,256]{4,3,2,1,0:T(8,128)S(1)} %slice_bitcast_fusion), channel_id=1, source_target_pairs={{0,8},{8,0},{16,24},{24,16},{32,40},{40,32},{48,56},{56,48},{64,72... | collective-permute-start | bytes 1179656 | tf_op jit(solution)/shard_map/ppermute | solution.py:164
  34.7 5.9 %collective-permute-start.5 = (bf16[4,3,8,256]{3,2,1,0:T(8,128)(2,1)S(1)}, bf16[4,3,8,256]{3,2,1,0:T(8,128)(2,1)S(1)}, u32[]{:S(2)}, u32[]{:S(2)}) collective-permute-start(bf16[4,3,8,256]{3,2,1,0:T(8,128)(2,1)S(1)} %get-tuple-element.15), channel_id=1, source_target_pairs={{0,16},{8,24},{16,0},{24,8},{32,48},{40,56},{48,32},{56,40},{64,80... | collective-permute-start | bytes 147464 | tf_op jit(solution)/shard_map/ppermute | solution.py:164
  37.8 5.6 %collective-permute-start.6 = (bf16[4,3,8,256]{3,2,1,0:T(8,128)(2,1)S(1)}, bf16[4,3,8,256]{3,2,1,0:T(8,128)(2,1)S(1)}, u32[]{:S(2)}, u32[]{:S(2)}) collective-permute-start(bf16[4,3,8,256]{3,2,1,0:T(8,128)(2,1)S(1)} %get-tuple-element.17), channel_id=1, source_target_pairs={{0,32},{8,40},{16,48},{24,56},{32,0},{40,8},{48,16},{56,24},{64,96... | collective-permute-start | bytes 147464 | tf_op jit(solution)/shard_map/ppermute | solution.py:164
  40.5 5.3 %collective-permute-start.7 = (bf16[4,3,8,256]{3,2,1,0:T(8,128)(2,1)S(1)}, bf16[4,3,8,256]{3,2,1,0:T(8,128)(2,1)S(1)}, u32[]{:S(2)}, u32[]{:S(2)}) collective-permute-start(bf16[4,3,8,256]{3,2,1,0:T(8,128)(2,1)S(1)} %get-tuple-element.16), channel_id=1, source_target_pairs={{0,48},{8,56},{16,32},{24,40},{32,16},{40,24},{48,0},{56,8},{64,11... | collective-permute-start | bytes 147464 | tf_op jit(solution)/shard_map/ppermute | solution.py:164
  45.9 5.4 %collective-permute-start.10 = (f32[3,8,256]{2,1,0:T(8,128)S(1)}, f32[3,8,256]{2,1,0:T(8,128)S(1)}, u32[]{:S(2)}, u32[]{:S(2)}) collective-permute-start(f32[3,8,256]{2,1,0:T(8,128)S(1)} %get-tuple-element.19), channel_id=1, source_target_pairs={{0,192},{8,200},{16,208},{24,216},{32,224},{40,232},{48,240},{56,2... | collective-permute-start | bytes 73736 | tf_op jit(solution)/shard_map/ppermute | solution.py:164
  47.6 3.8 %collective-permute-start.8 = (f32[3,8,256]{2,1,0:T(8,128)S(1)}, f32[3,8,256]{2,1,0:T(8,128)S(1)}, u32[]{:S(2)}, u32[]{:S(2)}) collective-permute-start(f32[3,8,256]{2,1,0:T(8,128)S(1)} %get-tuple-element.18), channel_id=1, source_target_pairs={{0,64},{8,72},{16,80},{24,88},{32,96},{40,104},{48,112},{56,120},{... | collective-permute-start | bytes 73736 | tf_op jit(solution)/shard_map/ppermute | solution.py:164
  48.8 5.3 %collective-permute-start.9 = (f32[3,8,256]{2,1,0:T(8,128)S(1)}, f32[3,8,256]{2,1,0:T(8,128)S(1)}, u32[]{:S(2)}, u32[]{:S(2)}) collective-permute-start(f32[3,8,256]{2,1,0:T(8,128)S(1)} %get-tuple-element.20), channel_id=1, source_target_pairs={{0,128},{8,136},{16,144},{24,152},{32,160},{40,168},{48,176},{56,1... | collective-permute-start | bytes 73736 | tf_op jit(solution)/shard_map/ppermute | solution.py:164
  54.2 6.8 %collective-permute-start.11 = (f32[8,256]{1,0:T(8,128)S(1)}, f32[8,256]{1,0:T(8,128)S(1)}, u32[]{:S(2)}, u32[]{:S(2)}) collective-permute-start(f32[8,256]{1,0:T(8,128)S(1)} %get-tuple-element.23), channel_id=1, source_target_pairs={{1,2},{3,4},{5,6},{2,1},{4,3},{6,5},{9,10},{11,12},{13,14},{10,9},... | collective-permute-start | bytes 24584 | tf_op jit(solution)/shard_map/ppermute | solution.py:193
  59.1 3.7 %collective-permute-start.12 = (f32[8,256]{1,0:T(8,128)S(1)}, f32[8,256]{1,0:T(8,128)S(1)}, u32[]{:S(2)}, u32[]{:S(2)}) collective-permute-start(f32[8,256]{1,0:T(8,128)S(1)} %get-tuple-element.22), channel_id=1, source_target_pairs={{0,1},{2,3},{4,5},{6,7},{1,0},{3,2},{5,4},{7,6},{8,9},{10,11},{12,... | collective-permute-start | bytes 24584 | tf_op jit(solution)/shard_map/ppermute | solution.py:192

commit v3 on v2

--- a/solution.py
+++ b/solution.py
@@ -19,8 +19,8 @@
 SM = pl.BlockSpec(memory_space=pltpu.SMEM)
 VM = pl.BlockSpec(memory_space=pltpu.VMEM)
 SUMS = (3 * PANELS + 1, TILE, BAND)
-X, Y = 4, 4
-TERMS = (2, X, Y, 3, 8, BAND)
+CHIPS = 16
+TERMS = (2, CHIPS, 3, 8, BAND)
 
 
 def vmem(mib):
@@ -84,44 +84,46 @@
     lax.fori_loop(0, (counts[which] + UNROLL - 1) // UNROLL, step, 0)
 
 
-def first_kernel(place, codes, counts, a_tiles, own, partner, sums):
+def first_kernel(codes, counts, a_tiles, own, partner, sums):
     def zero(i, carry):
         sums[i] = jnp.zeros((TILE, BAND), F32)
         return carry
 
     lax.fori_loop(0, 3 * PANELS + 1, zero, 0)
     apply_tiles(1, codes, counts, a_tiles, own, sums)
-    apply_tiles(2 - 2 * (place[0] & 1), codes, counts, a_tiles, partner, sums)
-
-
-def put_term(row, turned, panels, slot, terms):
+    apply_tiles(2 - 2 * (lax.axis_index("row") & 1), codes, counts, a_tiles, partner, sums)
+
+
+def put_term(turned, panels, slot, terms):
+    here = lax.axis_index("row") & 1
     term = jnp.dot(turned, panels[...].reshape(PANELS * TILE, BAND), preferred_element_type=F32).T
     for block in range(BAND // 8):
-        to = row ^ block
-        terms[to & 1, (to >> 1) & 3, to >> 3, slot] = term[block * 8:(block + 1) * 8]
-
-
-def second_kernel(place, codes, counts, a_tiles, other, before, own, sums, turned, terms):
-    apply_tiles(2 * (place[0] & 1), codes, counts, a_tiles, other, sums)
+        core = (0, block & 1, 1)[slot]
+        unit = 2 if slot == 1 else block & 1
+        terms[here ^ core, block >> 1, unit] = term[block * 8:(block + 1) * 8]
+
+
+def second_kernel(codes, counts, a_tiles, other, before, own, sums, turned, terms):
+    apply_tiles(2 * (lax.axis_index("row") & 1), codes, counts, a_tiles, other, sums)
     for k in range(3 * PANELS):
         lanes = pl.ds((k % PANELS) * TILE, TILE)
         turned[k // PANELS, :, lanes] = sums[k].astype(BF).T
-    put_term(place[0], turned[1], own, 1, terms)
-
-
-def first_sums(place, codes, counts, a_tiles, own, partner):
+    put_term(turned[1], own, 1, terms)
+
+
+def first_sums(codes, counts, a_tiles, own, partner):
     return pl.pallas_call(
         first_kernel,
         out_shape=jax.ShapeDtypeStruct(SUMS, F32),
-        in_specs=[SM] * 3 + [VM] * 3,
+        in_specs=[SM] * 2 + [VM] * 3,
         out_specs=VM,
         compiler_params=vmem(20),
         name="first_sums",
         cost_estimate=cost(10 * 10**9, 16 * 2**20),
-    )(place, codes, counts, a_tiles, own, partner)
-
-
-def second_sums(place, codes, counts, a_tiles, other, before, own):
+    )(codes, counts, a_tiles, own, partner)
+
+
+def second_sums(codes, counts, a_tiles, other, before, own):
     return pl.pallas_call(
         second_kernel,
         out_shape=(
@@ -129,40 +131,31 @@
             jax.ShapeDtypeStruct((3, BAND, PANELS * TILE), BF),
             jax.ShapeDtypeStruct(TERMS, F32),
         ),
-        in_specs=[SM] * 3 + [VM] * 4,
+        in_specs=[SM] * 2 + [VM] * 4,
         out_specs=(VM, VM, VM),
-        input_output_aliases={5: 0},
+        input_output_aliases={4: 0},
         compiler_params=vmem(24),
         name="second_sums",
         cost_estimate=cost(10 * 10**9, 16 * 2**20),
-    )(place, codes, counts, a_tiles, other, before, own)[1:]
-
-
-def couple_kernel(place, turned, even, odd, before, terms):
-    even_offset = place[1]
-    put_term(place[0], turned[even_offset], even, 0, terms)
-    put_term(place[0], turned[2 - even_offset], odd, 2, terms)
-
-
-def couple(place, turned, even, odd, before):
-    return pl.pallas_call(
-        couple_kernel,
+    )(codes, counts, a_tiles, other, before, own)[1:]
+
+
+def couple_kernel(turned, panels, before, terms, *, slot):
+    next_band = 2 - 2 * (lax.axis_index("col") & 1)
+    put_term(turned[next_band if slot == 0 else 2 - next_band], panels, slot, terms)
+
+
+def couple(turned, panels, before, slot):
+    return pl.pallas_call(
+        functools.partial(couple_kernel, slot=slot),
         out_shape=jax.ShapeDtypeStruct(TERMS, F32),
-        in_specs=[SM] + [VM] * 4,
+        in_specs=[VM] * 3,
         out_specs=VM,
-        input_output_aliases={4: 0},
+        input_output_aliases={2: 0},
         compiler_params=vmem(12),
-        name="couple",
+        name="couple%d" % slot,
         cost_estimate=cost(10**9, 6 * 2**20),
-    )(place, turned, even, odd, before)
-
-
-def swap_sum(value, shift, kind):
-    total = value[0]
-    for i in range(1, value.shape[0]):
-        pairs = [(r, r ^ (i << shift)) for r in range(2 * X * Y)]
-        total = total + lax.ppermute(value[i].astype(kind), "row", pairs).astype(F32)
-    return total
+    )(turned, panels, before)
 
 
 def both_ways(pairs):
@@ -178,22 +171,38 @@
     bridges = both_ways([(i, i + 1) for i in range(1, n_row - 1, 2)])
     even = lax.ppermute(p_panels, "col", even_pairs)
     odd = lax.ppermute(p_panels, "col", odd_pairs)
-    other = lax.ppermute(p_panels, "row", bridges)
-    partner = lax.ppermute(p_panels, "row", chip)
     low_col = (col & 1) == 0
-    place = jnp.stack([row, jnp.where(low_col, 2, 0)]).astype(jnp.int32)
-    codes, counts = plan(a_rows, a_cols, a_count)
-    before = first_sums(place, codes, counts, a_tiles, p_panels, partner)
-    turned, terms = second_sums(place, codes, counts, a_tiles, other, before, p_panels)
-    terms = couple(place, turned, even, odd, terms)
-    terms = swap_sum(terms, 0, F32)
-    terms = swap_sum(terms, 1, BF)
-    terms = swap_sum(terms, 3, F32)
-    from_even = lax.ppermute(terms[0], "col", even_pairs)
-    from_odd = lax.ppermute(terms[2], "col", odd_pairs)
+    def sums(_):
+        other = lax.ppermute(p_panels, "row", bridges)
+        partner = lax.ppermute(p_panels, "row", chip)
+        codes, counts = plan(a_rows, a_cols, a_count)
+        before = first_sums(codes, counts, a_tiles, p_panels, partner)
+        turned, terms = second_sums(codes, counts, a_tiles, other, before, p_panels)
+        return turned, terms
+
+    def nothing(_):
+        return jnp.zeros((3, BAND, PANELS * TILE), BF), jnp.zeros(TERMS, F32)
+
+    turned, terms = lax.cond(row < n_row, sums, nothing, 0)
+    terms = couple(turned, even, terms, 0)
+    terms = couple(turned, odd, terms, 2)
+    terms = terms[0] + lax.ppermute(terms[1], "row", chip)
+    groups = [list(range(c, n_row, 2)) for c in range(2)]
+    terms = lax.all_to_all(terms.astype(BF), "row", 0, 0, axis_index_groups=groups).astype(F32).sum(0)
+    pairs = [
+        (r * n_col + i, r * n_col + j)
+        for r in range(n_row)
+        for i, j in (odd_pairs if r & 1 else even_pairs)
+    ]
+    got = lax.ppermute(terms[:2], ("row", "col"), pairs)
+    first_core = (row & 1) == 0
+    kept = jnp.where(first_core, got[0], got[1])
+    given = lax.ppermute(jnp.where(first_core, got[1], got[0]), "row", chip)
+    from_even = jnp.where(first_core, kept, given)
+    from_odd = jnp.where(first_core, given, kept)
     lower = jnp.where(low_col, from_odd, from_even)
     upper = jnp.where(low_col, from_even, from_odd)
-    return jnp.concatenate([lower, terms[1], upper], axis=1)[None]
+    return jnp.concatenate([lower, terms[2], upper], axis=1)[None]
 
 
 def solution(mesh):

time: 63.7 us -> 55.2 us (0.87)
  the two profiles are of different devices: /device:TPU:96 before, /device:TPU:1 now
where the time goes in v3:
time: 55.2 us; the launch traced here: 55 us
  starting transfers between devices  19.8 us (36%)
  blocking collectives  13.7 us (25%)
  Pallas kernels  10.7 us (19%)
  waiting for transfers between devices  9.48 us (17%)
  other arithmetic  0.71 us (1%)
    all_to_all x1, blocking collectives, local(): lax.all_to_all(terms.astype(BF), 'row', 0, 0, axis_index_groups=groups)  13.7 us
    ppermute x1, starting transfers between devices, local(): given = lax.ppermute(jnp.where(first_core, got[1], got[0]), 'row', chip)  9.65 us
    ppermute x1, waiting for transfers between devices, sums(): other = lax.ppermute(p_panels, 'row', bridges)  6.62 us
    pallas_call x1, Pallas kernels, first_sums(): pl.pallas_call(first_kernel, out_shape=jax.ShapeDtypeStruct(SUMS, F32), i...  3.33 us
    pallas_call x1, Pallas kernels, plan(): pl.pallas_call(plan_kernel, out_shape=(jax.ShapeDtypeStruct((3 * LIST + 1...  3.26 us
    pallas_call x1, Pallas kernels, second_sums(): pl.pallas_call(second_kernel, out_shape=(jax.ShapeDtypeStruct(SUMS, F32),...  3.07 us
    ppermute x1, starting transfers between devices, sums(): other = lax.ppermute(p_panels, 'row', bridges)  3.02 us
    ppermute x1, starting transfers between devices, local(): even = lax.ppermute(p_panels, 'col', even_pairs)  2.47 us
  transfers between devices with their start and end apart: 7, of which 4 were waited for; matrix products, arithmetic and copies ran while one was open for 0% of the time, Pallas kernels for 18%

profile of v3, /device:TPU:1, one launch (start us, length us, event | category | flops | bytes accessed | tf_op | source)
XLA Modules:
  0.0 55.0 jit_solution(17094598727254863059)
XLA Ops:
  0.0 2.5 %collective-permute-start.3 = (bf16[16,128,256]{2,1,0:T(8,128)(2,1)}, bf16[16,128,256]{2,1,0:T(8,128)(2,1)S(1)}, u32[]{:S(2)}, u32[]{:S(2)}) collective-permute-start(bf16[16,128,256]{2,1,0:T(8,128)(2,1)} %param.11), channel_id=1, source_target_pairs={{0,1},{2,3},{4,5},{6,7},{1,0},{3,2},{5,4},{7,6},{8,9},{10,11},{12,... | collective-permute-start | bytes 3145736 | tf_op jit(solution)/shard_map/ppermute | solution.py:172
  2.5 0.7 %collective-permute-start.2 = (bf16[16,128,256]{2,1,0:T(8,128)(2,1)}, bf16[16,128,256]{2,1,0:T(8,128)(2,1)S(1)}, u32[]{:S(2)}, u32[]{:S(2)}) collective-permute-start(bf16[16,128,256]{2,1,0:T(8,128)(2,1)} %param.11), channel_id=1, source_target_pairs={{1,2},{3,4},{5,6},{2,1},{4,3},{6,5},{9,10},{11,12},{13,14},{10,9},... | collective-permute-start | bytes 3145736 | tf_op jit(solution)/shard_map/ppermute | solution.py:173
  3.2 20.7 %conditional.1 = (bf16[3,256,2048]{2,1,0:T(8,128)(2,1)S(1)}, f32[2,16,3,8,256]{4,3,2,1,0:T(8,128)S(1)}) conditional(s32[]{:T(128)} %convert_element_type.9, () %tuple.13, (s32[1,256]{1,0:T(1,128)}, s32[1,256]{1,0:T(1,128)}, s32[1,1]{1,0:T(1,128)}, bf16[16,128,256]{2,1,0:T(8,128)(2,1)}, bf16[1,256,128,128]{3,2,1,0:T(8,128)(2,1)}) %tuple.14), branch_computations={%region_0.0_spmd, %region_1.0_spmd} | conditional | flops 49999998976 | bytes 79701928 | solution.py:186
  3.2 1.0 %collective-permute-start.1 = (bf16[16,128,256]{2,1,0:T(8,128)(2,1)}, bf16[16,128,256]{2,1,0:T(8,128)(2,1)S(1)}, u32[]{:S(2)}, u32[]{:S(2)}) collective-permute-start(bf16[16,128,256]{2,1,0:T(8,128)(2,1)} %get-tuple-element.21.own), channel_id=1, source_target_pairs={{0,8},{16,24},{32,40},{48,56},{64,72},{80,88},{96,104},{112,120},{... | collective-permute-start | bytes 3145736 | tf_op jit(solution)/shard_map/cond/branch_1_fun/ppermute | solution.py:177
  4.2 3.0 %collective-permute-start = (bf16[16,128,256]{2,1,0:T(8,128)(2,1)}, bf16[16,128,256]{2,1,0:T(8,128)(2,1)S(1)}, u32[]{:S(2)}, u32[]{:S(2)}) collective-permute-start(bf16[16,128,256]{2,1,0:T(8,128)(2,1)} %get-tuple-element.21.own), channel_id=1, source_target_pairs={{8,16},{24,32},{40,48},{56,64},{72,80},{88,96},{104,112},{120,128}... | collective-permute-start | bytes 3145736 | tf_op jit(solution)/shard_map/cond/branch_1_fun/ppermute | solution.py:176
  7.3 3.3 %plan.1 = (s32[817]{0:T(1024)S(1)}, s32[3]{0:T(128)S(1)}) custom-call(s32[1,256]{1,0:T(1,128)} %get-tuple-element.32.rows, s32[1,256]{1,0:T(1,128)} %get-tuple-element.33.cols, s32[1,1]{1,0:T(1,128)} %get-tuple-element.34.count), custom_call_target="tpu_custom_call" | custom-call | flops 30000001024 | bytes 10000 | tf_op jit(solution)/shard_map/cond/branch_1_fun/plan/pallas_call | solution.py:58
  10.6 0.0 collective-permute-done.1.partner
  10.6 0.1 copy-done
  10.7 0.2 copy-done.1
  10.9 3.3 %first_sums.1.before = f32[49,128,256]{2,1,0:T(8,128)S(1)} custom-call(s32[817]{0:T(1024)S(1)} %get-tuple-element.18.codes, s32[3]{0:T(128)S(1)} %get-tuple-element.19.counts, bf16[1,256,128,128]{3,2,1,0:T(8,128)(2,1)S(1)} %copy-done, bf16[16,128,256]{2,1,0:T(8,128)(2,1)S(1)} %copy-done.1, bf16[16,128,256]{2,1,0:T(8,128)(2,1)S(1)} %collective-permute-done.1.partner), custom_call_target="tpu_custom_call" | custom-call | flops 10000000000 | bytes 16777216 | tf_op jit(solution)/shard_map/cond/branch_1_fun/first_sums/pallas_call | solution.py:115
  14.2 6.6 %collective-permute-done.other = bf16[16,128,256]{2,1,0:T(8,128)(2,1)S(1)} collective-permute-done((bf16[16,128,256]{2,1,0:T(8,128)(2,1)}, bf16[16,128,256]{2,1,0:T(8,128)(2,1)S(1)}, u32[]{:S(2)}, u32[]{:S(2)}) %collective-permute-start) | collective-permute-done | bytes 1048608 | tf_op jit(solution)/shard_map/cond/branch_1_fun/ppermute | solution.py:176
  20.9 3.1 %second_sums.1 = (f32[49,128,256]{2,1,0:T(8,128)S(1)}, bf16[3,256,2048]{2,1,0:T(8,128)(2,1)S(1)}, f32[2,16,3,8,256]{4,3,2,1,0:T(8,128)S(1)}) custom-call(s32[817]{0:T(1024)S(1)} %get-tuple-element.18.codes, s32[3]{0:T(128)S(1)} %get-tuple-element.19.counts, bf16[1,256,128,128]{3,2,1,0:T(8,128)(2,1)S(1)} %copy-done, ...), custom_call_target="tpu_custom_call", output_to_operand_aliasing={{0}: (4, {})} | custom-call | flops 10000000000 | bytes 16777216 | tf_op jit(solution)/shard_map/cond/branch_1_fun/second_sums/pallas_call | solution.py:127
  23.9 0.7 %collective-permute-done.3.panels = bf16[16,128,256]{2,1,0:T(8,128)(2,1)S(1)} collective-permute-done((bf16[16,128,256]{2,1,0:T(8,128)(2,1)}, bf16[16,128,256]{2,1,0:T(8,128)(2,1)S(1)}, u32[]{:S(2)}, u32[]{:S(2)}) %collective-permute-start.3) | collective-permute-done | bytes 1048608 | tf_op jit(solution)/shard_map/ppermute | solution.py:172
  24.6 0.5 couple0.1.before
  25.1 0.0 collective-permute-done.2.panels
  25.1 0.5 couple2.1
  25.7 2.3 %collective-permute-start.4 = (f32[16,3,8,256]{3,2,1,0:T(8,128)S(1)}, f32[16,3,8,256]{3,2,1,0:T(8,128)S(1)}, u32[]{:S(2)}, u32[]{:S(2)}) collective-permute-start(f32[16,3,8,256]{3,2,1,0:T(8,128)S(1)} %slice_bitcast_fusion), channel_id=1, source_target_pairs={{0,8},{16,24},{32,40},{48,56},{64,72},{80,88},{96,104},{112,120},{... | collective-permute-start | bytes 1179656 | tf_op jit(solution)/shard_map/ppermute | solution.py:189
  28.0 1.3 %collective-permute-done.4 = f32[16,3,8,256]{3,2,1,0:T(8,128)S(1)} collective-permute-done((f32[16,3,8,256]{3,2,1,0:T(8,128)S(1)}, f32[16,3,8,256]{3,2,1,0:T(8,128)S(1)}, u32[]{:S(2)}, u32[]{:S(2)}) %collective-permute-start.4) | collective-permute-done | bytes 393248 | tf_op jit(solution)/shard_map/ppermute | solution.py:189
  29.3 0.1 fusion.1
  29.4 13.7 %all_to_all.5 = bf16[16,3,8,256]{3,2,1,0:T(8,128)(2,1)S(1)} all-to-all(bf16[16,3,8,256]{3,2,1,0:T(8,128)(2,1)S(1)} %fusion.1), channel_id=1, replica_groups={{0,16,32,48,64,80,96,112,128,144,160,176,192,208,224,240},{8,24,40,56,7..., dimensions={0} | all-to-all | bytes 393216 | tf_op jit(solution)/shard_map/all_to_all | solution.py:191
  43.2 0.7 %collective-permute-start.5 = (f32[2,8,256]{2,1,0:T(8,128)S(1)}, f32[2,8,256]{2,1,0:T(8,128)S(1)}, u32[]{:S(2)}, u32[]{:S(2)}) collective-permute-start(f32[2,8,256]{2,1,0:T(8,128)S(1)} %slice.28), channel_id=1, source_target_pairs={{0,1},{2,3},{4,5},{6,7},{1,0},{3,2},{5,4},{7,6},{9,10},{11,12},{13... | collective-permute-start | bytes 49160 | tf_op jit(solution)/shard_map/ppermute | solution.py:197
  43.9 9.6 %collective-permute-start.6 = (f32[8,256]{1,0:T(8,128)S(1)}, f32[8,256]{1,0:T(8,128)S(1)}, u32[]{:S(2)}, u32[]{:S(2)}) collective-permute-start(f32[8,256]{1,0:T(8,128)S(1)} %select_bitcast_fusion), channel_id=1, source_target_pairs={{0,8},{16,24},{32,40},{48,56},{64,72},{80,88},{96,104},{112,120},{... | collective-permute-start | bytes 24584 | tf_op jit(solution)/shard_map/ppermute | solution.py:200
  53.5 0.8 %collective-permute-done.6 = f32[8,256]{1,0:T(8,128)S(1)} collective-permute-done((f32[8,256]{1,0:T(8,128)S(1)}, f32[8,256]{1,0:T(8,128)S(1)}, u32[]{:S(2)}, u32[]{:S(2)}) %collective-permute-start.6) | collective-permute-done | bytes 8224 | tf_op jit(solution)/shard_map/ppermute | solution.py:200
  54.3 0.6 %maximum_bitcast_fusion = f32[1,8,768]{2,1,0:T(8,128)} fusion(f32[8,256]{1,0:T(8,128)S(1)} %get-tuple-element.37, f32[8,256]{1,0:T(8,128)S(1)} %slice_bitcast_fusion.2, f32[8,256]{1,0:T(8,128)S(1)} %get-tuple-element.36), kind=kLoop, calls=%fused_computation.5 | loop fusion | flops 12288 | bytes 49152 | tf_op jit(solution)/shard_map/broadcast_in_dim | solution.py:205
  (9 shorter events, 0.1 us)
Async XLA Ops:
  0.0 24.6 %collective-permute-start.3 = (bf16[16,128,256]{2,1,0:T(8,128)(2,1)}, bf16[16,128,256]{2,1,0:T(8,128)(2,1)S(1)}, u32[]{:S(2)}, u32[]{:S(2)}) collective-permute-start(bf16[16,128,256]{2,1,0:T(8,128)(2,1)} %param.11), channel_id=1, source_target_pairs={{0,1},{2,3},{4,5},{6,7},{1,0},{3,2},{5,4},{7,6},{8,9},{10,11},{12,... | collective-permute-start | bytes 3145736 | tf_op jit(solution)/shard_map/ppermute | solution.py:172
  2.5 22.7 %collective-permute-start.2 = (bf16[16,128,256]{2,1,0:T(8,128)(2,1)}, bf16[16,128,256]{2,1,0:T(8,128)(2,1)S(1)}, u32[]{:S(2)}, u32[]{:S(2)}) collective-permute-start(bf16[16,128,256]{2,1,0:T(8,128)(2,1)} %param.11), channel_id=1, source_target_pairs={{1,2},{3,4},{5,6},{2,1},{4,3},{6,5},{9,10},{11,12},{13,14},{10,9},... | collective-permute-start | bytes 3145736 | tf_op jit(solution)/shard_map/ppermute | solution.py:173
  3.2 7.4 %collective-permute-start.1 = (bf16[16,128,256]{2,1,0:T(8,128)(2,1)}, bf16[16,128,256]{2,1,0:T(8,128)(2,1)S(1)}, u32[]{:S(2)}, u32[]{:S(2)}) collective-permute-start(bf16[16,128,256]{2,1,0:T(8,128)(2,1)} %get-tuple-element.21.own), channel_id=1, source_target_pairs={{0,8},{16,24},{32,40},{48,56},{64,72},{80,88},{96,104},{112,120},{... | collective-permute-start | bytes 3145736 | tf_op jit(solution)/shard_map/cond/branch_1_fun/ppermute | solution.py:177
  4.2 16.6 %collective-permute-start = (bf16[16,128,256]{2,1,0:T(8,128)(2,1)}, bf16[16,128,256]{2,1,0:T(8,128)(2,1)S(1)}, u32[]{:S(2)}, u32[]{:S(2)}) collective-permute-start(bf16[16,128,256]{2,1,0:T(8,128)(2,1)} %get-tuple-element.21.own), channel_id=1, source_target_pairs={{8,16},{24,32},{40,48},{56,64},{72,80},{88,96},{104,112},{120,128}... | collective-permute-start | bytes 3145736 | tf_op jit(solution)/shard_map/cond/branch_1_fun/ppermute | solution.py:176
  7.3 3.4 %copy-start = (bf16[1,256,128,128]{3,2,1,0:T(8,128)(2,1)S(1)}, bf16[1,256,128,128]{3,2,1,0:T(8,128)(2,1)}, u32[]{:S(2)}) copy-start(bf16[1,256,128,128]{3,2,1,0:T(8,128)(2,1)} %get-tuple-element.35.a_tiles) | copy-start | bytes 25165828 | tf_op jit(solution)/shard_map/cond
  7.3 3.6 %copy-start.1 = (bf16[16,128,256]{2,1,0:T(8,128)(2,1)S(1)}, bf16[16,128,256]{2,1,0:T(8,128)(2,1)}, u32[]{:S(2)}) copy-start(bf16[16,128,256]{2,1,0:T(8,128)(2,1)} %get-tuple-element.21.own) | copy-start | bytes 3145732 | tf_op jit(solution)/shard_map/cond
  25.7 3.6 %collective-permute-start.4 = (f32[16,3,8,256]{3,2,1,0:T(8,128)S(1)}, f32[16,3,8,256]{3,2,1,0:T(8,128)S(1)}, u32[]{:S(2)}, u32[]{:S(2)}) collective-permute-start(f32[16,3,8,256]{3,2,1,0:T(8,128)S(1)} %slice_bitcast_fusion), channel_id=1, source_target_pairs={{0,8},{16,24},{32,40},{48,56},{64,72},{80,88},{96,104},{112,120},{... | collective-permute-start | bytes 1179656 | tf_op jit(solution)/shard_map/ppermute | solution.py:189
  43.2 0.7 %collective-permute-start.5 = (f32[2,8,256]{2,1,0:T(8,128)S(1)}, f32[2,8,256]{2,1,0:T(8,128)S(1)}, u32[]{:S(2)}, u32[]{:S(2)}) collective-permute-start(f32[2,8,256]{2,1,0:T(8,128)S(1)} %slice.28), channel_id=1, source_target_pairs={{0,1},{2,3},{4,5},{6,7},{1,0},{3,2},{5,4},{7,6},{9,10},{11,12},{13... | collective-permute-start | bytes 49160 | tf_op jit(solution)/shard_map/ppermute | solution.py:197
  43.9 10.5 %collective-permute-start.6 = (f32[8,256]{1,0:T(8,128)S(1)}, f32[8,256]{1,0:T(8,128)S(1)}, u32[]{:S(2)}, u32[]{:S(2)}) collective-permute-start(f32[8,256]{1,0:T(8,128)S(1)} %select_bitcast_fusion), channel_id=1, source_target_pairs={{0,8},{16,24},{32,40},{48,56},{64,72},{80,88},{96,104},{112,120},{... | collective-permute-start | bytes 24584 | tf_op jit(solution)/shard_map/ppermute | solution.py:200

commit v4 on v3

--- a/solution.py
+++ b/solution.py
@@ -20,7 +20,8 @@
 VM = pl.BlockSpec(memory_space=pltpu.VMEM)
 SUMS = (3 * PANELS + 1, TILE, BAND)
 CHIPS = 16
-TERMS = (2, CHIPS, 3, 8, BAND)
+TERMS = (CHIPS, 16, BAND)
+TURNED = (BAND, PANELS * TILE)
 
 
 def vmem(mib):
@@ -94,21 +95,25 @@
     apply_tiles(2 - 2 * (lax.axis_index("row") & 1), codes, counts, a_tiles, partner, sums)
 
 
-def put_term(turned, panels, slot, terms):
-    here = lax.axis_index("row") & 1
-    term = jnp.dot(turned, panels[...].reshape(PANELS * TILE, BAND), preferred_element_type=F32).T
-    for block in range(BAND // 8):
-        core = (0, block & 1, 1)[slot]
-        unit = 2 if slot == 1 else block & 1
-        terms[here ^ core, block >> 1, unit] = term[block * 8:(block + 1) * 8]
-
-
-def second_kernel(codes, counts, a_tiles, other, before, own, sums, turned, terms):
-    apply_tiles(2 * (lax.axis_index("row") & 1), codes, counts, a_tiles, other, sums)
-    for k in range(3 * PANELS):
-        lanes = pl.ds((k % PANELS) * TILE, TILE)
-        turned[k // PANELS, :, lanes] = sums[k].astype(BF).T
-    put_term(turned[1], own, 1, terms)
+def term_of(turned, panels):
+    rows = panels[...].reshape(PANELS * TILE, BAND)
+    return jnp.dot(turned[...], rows, preferred_element_type=F32)
+
+
+def by_chip(term):
+    return term.T.reshape(TERMS).astype(BF)
+
+
+def second_kernel(
+    codes, counts, a_tiles, other, before, own, sums, mine, theirs, terms, turned
+):
+    core = lax.axis_index("row") & 1
+    apply_tiles(2 * core, codes, counts, a_tiles, other, sums)
+    offset = 2 * (1 - ((lax.axis_index("col") ^ core) & 1))
+    for part, ref in ((offset, mine), (2 - offset, theirs), (1, turned)):
+        for k in range(PANELS):
+            ref[:, pl.ds(k * TILE, TILE)] = sums[part * PANELS + k].astype(BF).T
+    terms[...] = by_chip(term_of(turned, own))
 
 
 def first_sums(codes, counts, a_tiles, own, partner):
@@ -128,11 +133,13 @@
         second_kernel,
         out_shape=(
             jax.ShapeDtypeStruct(SUMS, F32),
-            jax.ShapeDtypeStruct((3, BAND, PANELS * TILE), BF),
-            jax.ShapeDtypeStruct(TERMS, F32),
+            jax.ShapeDtypeStruct(TURNED, BF),
+            jax.ShapeDtypeStruct(TURNED, BF),
+            jax.ShapeDtypeStruct(TERMS, BF),
         ),
         in_specs=[SM] * 2 + [VM] * 4,
-        out_specs=(VM, VM, VM),
+        out_specs=(VM, VM, VM, VM),
+        scratch_shapes=[pltpu.VMEM(TURNED, BF)],
         input_output_aliases={4: 0},
         compiler_params=vmem(24),
         name="second_sums",
@@ -140,22 +147,38 @@
     )(codes, counts, a_tiles, other, before, own)[1:]
 
 
-def couple_kernel(turned, panels, before, terms, *, slot):
-    next_band = 2 - 2 * (lax.axis_index("col") & 1)
-    put_term(turned[next_band if slot == 0 else 2 - next_band], panels, slot, terms)
-
-
-def couple(turned, panels, before, slot):
-    return pl.pallas_call(
-        functools.partial(couple_kernel, slot=slot),
-        out_shape=jax.ShapeDtypeStruct(TERMS, F32),
-        in_specs=[VM] * 3,
+def partner_kernel(received, cross, part):
+    part[...] = term_of(received, cross)
+
+
+def partner_term(received, cross):
+    return pl.pallas_call(
+        partner_kernel,
+        out_shape=jax.ShapeDtypeStruct((BAND, BAND), F32),
+        in_specs=[VM] * 2,
         out_specs=VM,
-        input_output_aliases={2: 0},
-        compiler_params=vmem(12),
-        name="couple%d" % slot,
+        compiler_params=vmem(8),
+        name="partner_term",
         cost_estimate=cost(10**9, 6 * 2**20),
-    )(turned, panels, before)
+    )(received, cross)
+
+
+def couple_kernel(mine, straight, part, own, out):
+    upper_band = (lax.axis_index("row") ^ lax.axis_index("col")) & 1
+    out[upper_band] = own[...]
+    out[1 - upper_band] = by_chip(term_of(mine, straight) + part[...])
+
+
+def couple(mine, straight, part, own):
+    return pl.pallas_call(
+        couple_kernel,
+        out_shape=jax.ShapeDtypeStruct((2,) + TERMS, BF),
+        in_specs=[VM] * 4,
+        out_specs=VM,
+        compiler_params=vmem(8),
+        name="couple",
+        cost_estimate=cost(10**9, 6 * 2**20),
+    )(mine, straight, part, own)
 
 
 def both_ways(pairs):
@@ -169,40 +192,50 @@
     odd_pairs = both_ways([(i, i + 1) for i in range(1, n_col - 1, 2)])
     chip = both_ways([(i, i + 1) for i in range(0, n_row - 1, 2)])
     bridges = both_ways([(i, i + 1) for i in range(1, n_row - 1, 2)])
-    even = lax.ppermute(p_panels, "col", even_pairs)
-    odd = lax.ppermute(p_panels, "col", odd_pairs)
     low_col = (col & 1) == 0
+    col_pairs = (even_pairs, odd_pairs)
+    straight = lax.ppermute(p_panels, ("row", "col"), [
+        (r * n_col + i, r * n_col + j) for r in range(n_row) for i, j in col_pairs[r & 1]
+    ])
+
     def sums(_):
         other = lax.ppermute(p_panels, "row", bridges)
         partner = lax.ppermute(p_panels, "row", chip)
+        cross = lax.ppermute(p_panels, ("row", "col"), [
+            (r * n_col + i, (r ^ 1) * n_col + j)
+            for r in range(n_row)
+            for i, j in col_pairs[1 - (r & 1)]
+        ])
         codes, counts = plan(a_rows, a_cols, a_count)
         before = first_sums(codes, counts, a_tiles, p_panels, partner)
-        turned, terms = second_sums(codes, counts, a_tiles, other, before, p_panels)
-        return turned, terms
+        mine, theirs, terms = second_sums(codes, counts, a_tiles, other, before, p_panels)
+        return mine, partner_term(lax.ppermute(theirs, "row", chip), cross), terms
 
     def nothing(_):
-        return jnp.zeros((3, BAND, PANELS * TILE), BF), jnp.zeros(TERMS, F32)
-
-    turned, terms = lax.cond(row < n_row, sums, nothing, 0)
-    terms = couple(turned, even, terms, 0)
-    terms = couple(turned, odd, terms, 2)
-    terms = terms[0] + lax.ppermute(terms[1], "row", chip)
-    groups = [list(range(c, n_row, 2)) for c in range(2)]
-    terms = lax.all_to_all(terms.astype(BF), "row", 0, 0, axis_index_groups=groups).astype(F32).sum(0)
-    pairs = [
-        (r * n_col + i, r * n_col + j)
-        for r in range(n_row)
-        for i, j in (odd_pairs if r & 1 else even_pairs)
+        return jnp.zeros(TURNED, BF), jnp.zeros((BAND, BAND), F32), jnp.zeros(TERMS, BF)
+
+    mine, part, terms = lax.cond(row < n_row, sums, nothing, 0)
+    both = couple(mine, straight, part, terms)
+    first_core = (row & 1) == 0
+    upper_band = ((row ^ col) & 1) == 1
+    groups = [
+        [(2 * i + core) * n_col + (c + k) % n_col for k in range(2) for i in range(CHIPS)]
+        for core in range(2)
+        for c in range(core, n_col, 2)
     ]
-    got = lax.ppermute(terms[:2], ("row", "col"), pairs)
-    first_core = (row & 1) == 0
-    kept = jnp.where(first_core, got[0], got[1])
-    given = lax.ppermute(jnp.where(first_core, got[1], got[0]), "row", chip)
-    from_even = jnp.where(first_core, kept, given)
-    from_odd = jnp.where(first_core, given, kept)
-    lower = jnp.where(low_col, from_odd, from_even)
-    upper = jnp.where(low_col, from_even, from_odd)
-    return jnp.concatenate([lower, terms[2], upper], axis=1)[None]
+    both = both.reshape((2 * CHIPS,) + TERMS[1:])
+    both = lax.all_to_all(both, ("row", "col"), 0, 0, axis_index_groups=groups)
+    lower, upper = both.reshape((2,) + TERMS).astype(F32).sum(1)
+    own = jnp.where(upper_band, upper, lower)
+    ends = jnp.where(upper_band, lower, upper)
+    mine = jnp.stack([own, ends]).reshape(2, 2, 8, BAND)
+    kept = jnp.where(first_core, mine[:, 0], mine[:, 1])
+    given = lax.ppermute(jnp.where(first_core, mine[:, 1], mine[:, 0]), "row", chip)
+    from_even = jnp.where(first_core, kept[1], given[1])
+    from_odd = jnp.where(first_core, given[1], kept[1])
+    left = jnp.where(low_col, from_odd, from_even)
+    right = jnp.where(low_col, from_even, from_odd)
+    return jnp.concatenate([left, kept[0] + given[0], right], axis=1)[None]
 
 
 def solution(mesh):

time: 55.2 us -> 52.5 us (0.951)
  blocking collectives: 13.7 us -> 0 us
  waiting for transfers between devices: 9.48 us -> 18.3 us
  starting transfers between devices: 19.8 us -> 22.1 us
    all_to_all x1 -> x0, blocking collectives: 13.7 us -> none  [local(): lax.all_to_all(terms.astype(BF), 'row', 0, 0, axis_index_groups=groups)]
    ppermute x5 -> x4, starting transfers between devices: 15.8 us -> 2.26 us  [the longest x1 1.36 us: sums(): lax.ppermute(p_panels, ('row', 'col'), [(r * n_col + i, (r ^ 1) * n_col +...]
    all_to_all x0 -> x1, starting transfers between devices: none -> 12.1 us  [local(): both = lax.all_to_all(both, ('row', 'col'), 0, 0, axis_index_groups=groups)]
    all_to_all x0 -> x1, waiting for transfers between devices: none -> 7.39 us  [local(): both = lax.all_to_all(both, ('row', 'col'), 0, 0, axis_index_groups=groups)]
    ppermute x1, starting transfers between devices: 1.04 us -> 4.69 us  [sums(): partner = lax.ppermute(p_panels, 'row', chip)]
    ppermute x5 -> x4, waiting for transfers between devices: 2.85 us -> 5.16 us  [the longest x1 3.99 us: sums(): lax.ppermute(p_panels, ('row', 'col'), [(r * n_col + i, (r ^ 1) * n_col +...]
    ppermute x1, waiting for transfers between devices: 6.62 us -> 5.72 us  [sums(): other = lax.ppermute(p_panels, 'row', bridges)]
    pallas_call x2, Pallas kernels: 1.02 us -> 1.65 us  [the longest x1 1.22 us: couple(): pl.pallas_call(couple_kernel, out_shape=jax.ShapeDtypeStruct((2,) + TERMS...]
  transfers between devices with their start and end apart: 7 -> 7, of which waited for: 4 -> 4; matrix products, arithmetic and copies ran while one was open for 0% -> 0% of each run, Pallas kernels for 18% -> 17%
where the time goes in v4:
time: 52.5 us; the launch traced here: 51.9 us
  starting transfers between devices  22.1 us (42%)
  waiting for transfers between devices  18.3 us (35%)
  Pallas kernels  10.2 us (19%)
  other arithmetic  0.67 us (1%)
  local copies, waits for them, and re-layouts  0.55 us (1%)
    all_to_all x1, starting transfers between devices, local(): both = lax.all_to_all(both, ('row', 'col'), 0, 0, axis_index_groups=groups)  12.1 us
    all_to_all x1, waiting for transfers between devices, local(): both = lax.all_to_all(both, ('row', 'col'), 0, 0, axis_index_groups=groups)  7.39 us
    ppermute x1, waiting for transfers between devices, sums(): other = lax.ppermute(p_panels, 'row', bridges)  5.72 us
    ppermute x1, starting transfers between devices, sums(): partner = lax.ppermute(p_panels, 'row', chip)  4.69 us
    ppermute x1, waiting for transfers between devices, sums(): lax.ppermute(p_panels, ('row', 'col'), [(r * n_col + i, (r ^ 1) * n_col +...  3.99 us
    pallas_call x1, Pallas kernels, plan(): pl.pallas_call(plan_kernel, out_shape=(jax.ShapeDtypeStruct((3 * LIST + 1...  3.04 us
    ppermute x1, starting transfers between devices, sums(): other = lax.ppermute(p_panels, 'row', bridges)  3.02 us
    pallas_call x1, Pallas kernels, first_sums(): pl.pallas_call(first_kernel, out_shape=jax.ShapeDtypeStruct(SUMS, F32), i...  2.86 us
  transfers between devices with their start and end apart: 7, of which 4 were waited for; matrix products, arithmetic and copies ran while one was open for 0% of the time, Pallas kernels for 17%

profile of v4, /device:TPU:1, one launch (start us, length us, event | category | flops | bytes accessed | tf_op | source)
XLA Modules:
  0.0 51.9 jit_solution(11960798695689457492)
XLA Ops:
  0.0 0.7 %collective-permute-start.4 = (bf16[16,128,256]{2,1,0:T(8,128)(2,1)}, bf16[16,128,256]{2,1,0:T(8,128)(2,1)S(1)}, u32[]{:S(2)}, u32[]{:S(2)}) collective-permute-start(bf16[16,128,256]{2,1,0:T(8,128)(2,1)} %param.11), channel_id=1, source_target_pairs={{0,1},{2,3},{4,5},{6,7},{1,0},{3,2},{5,4},{7,6},{9,10},{11,12},{13... | collective-permute-start | bytes 3145736 | tf_op jit(solution)/shard_map/ppermute | solution.py:197
  0.7 28.5 %conditional.1 = (bf16[256,2048]{1,0:T(8,128)(2,1)S(1)}, f32[256,256]{1,0:T(8,128)S(1)}, bf16[16,16,256]{2,1,0:T(8,128)(2,1)S(1)}) conditional(s32[]{:T(128)} %convert_element_type.9, () %tuple.13, (s32[1,256]{1,0:T(1,128)}, s32[1,256]{1,0:T(1,128)}, s32[1,1]{1,0:T(1,128)}, bf16[16,128,256]{2,1,0:T(8,128)(2,1)}, ...), branch_computations={%region_0.0_spmd, %region_1.0_spmd} | conditional | flops 51000000512 | bytes 94382080 | solution.py:217
  0.7 4.7 %collective-permute-start.1 = (bf16[16,128,256]{2,1,0:T(8,128)(2,1)}, bf16[16,128,256]{2,1,0:T(8,128)(2,1)S(1)}, u32[]{:S(2)}, u32[]{:S(2)}) collective-permute-start(bf16[16,128,256]{2,1,0:T(8,128)(2,1)} %get-tuple-element.21.own), channel_id=1, source_target_pairs={{0,8},{16,24},{32,40},{48,56},{64,72},{80,88},{96,104},{112,120},{... | collective-permute-start | bytes 3145736 | tf_op jit(solution)/shard_map/cond/branch_1_fun/ppermute | solution.py:203
  5.4 3.0 %collective-permute-start = (bf16[16,128,256]{2,1,0:T(8,128)(2,1)}, bf16[16,128,256]{2,1,0:T(8,128)(2,1)S(1)}, u32[]{:S(2)}, u32[]{:S(2)}) collective-permute-start(bf16[16,128,256]{2,1,0:T(8,128)(2,1)} %get-tuple-element.21.own), channel_id=1, source_target_pairs={{8,16},{24,32},{40,48},{56,64},{72,80},{88,96},{104,112},{120,128}... | collective-permute-start | bytes 3145736 | tf_op jit(solution)/shard_map/cond/branch_1_fun/ppermute | solution.py:202
  8.5 1.4 %collective-permute-start.3 = (bf16[16,128,256]{2,1,0:T(8,128)(2,1)}, bf16[16,128,256]{2,1,0:T(8,128)(2,1)S(1)}, u32[]{:S(2)}, u32[]{:S(2)}) collective-permute-start(bf16[16,128,256]{2,1,0:T(8,128)(2,1)} %get-tuple-element.21.own), channel_id=1, source_target_pairs={{1,10},{3,12},{5,14},{2,9},{4,11},{6,13},{8,1},{10,3},{12,5},{14,7... | collective-permute-start | bytes 3145736 | tf_op jit(solution)/shard_map/cond/branch_1_fun/ppermute | solution.py:204
  9.8 0.0 copy-start
  9.8 3.0 %plan.1 = (s32[817]{0:T(1024)S(1)}, s32[3]{0:T(128)S(1)}) custom-call(s32[1,256]{1,0:T(1,128)} %get-tuple-element.35.rows, s32[1,256]{1,0:T(1,128)} %get-tuple-element.36.cols, s32[1,1]{1,0:T(1,128)} %get-tuple-element.37.count), custom_call_target="tpu_custom_call" | custom-call | flops 30000001024 | bytes 10000 | tf_op jit(solution)/shard_map/cond/branch_1_fun/plan/pallas_call | solution.py:59
  12.9 0.0 collective-permute-done.1.partner
  12.9 0.3 copy-done
  13.2 0.2 copy-done.1
  13.4 2.9 %first_sums.1.before = f32[49,128,256]{2,1,0:T(8,128)S(1)} custom-call(s32[817]{0:T(1024)S(1)} %get-tuple-element.18.codes, s32[3]{0:T(128)S(1)} %get-tuple-element.19.counts, bf16[1,256,128,128]{3,2,1,0:T(8,128)(2,1)S(1)} %copy-done, bf16[16,128,256]{2,1,0:T(8,128)(2,1)S(1)} %copy-done.1, bf16[16,128,256]{2,1,0:T(8,128)(2,1)S(1)} %collective-permute-done.1.partner), custom_call_target="tpu_custom_call" | custom-call | flops 10000000000 | bytes 16777216 | tf_op jit(solution)/shard_map/cond/branch_1_fun/first_sums/pallas_call | solution.py:120
  16.3 5.7 %collective-permute-done.other = bf16[16,128,256]{2,1,0:T(8,128)(2,1)S(1)} collective-permute-done((bf16[16,128,256]{2,1,0:T(8,128)(2,1)}, bf16[16,128,256]{2,1,0:T(8,128)(2,1)S(1)}, u32[]{:S(2)}, u32[]{:S(2)}) %collective-permute-start) | collective-permute-done | bytes 1048608 | tf_op jit(solution)/shard_map/cond/branch_1_fun/ppermute | solution.py:202
  22.0 2.6 %second_sums.1 = (f32[49,128,256]{2,1,0:T(8,128)S(1)}, bf16[256,2048]{1,0:T(8,128)(2,1)S(1)}, bf16[256,2048]{1,0:T(8,128)(2,1)S(1)}, bf16[16,16,256]{2,1,0:T(8,128)(2,1)S(1)}) custom-call(s32[817]{0:T(1024)S(1)} %get-tuple-element.18.codes, s32[3]{0:T(128)S(1)} %get-tuple-element.19.counts, ...), custom_call_target="tpu_custom_call", output_to_operand_aliasing={{0}: (4, {})} | custom-call | flops 10000000000 | bytes 16777216 | tf_op jit(solution)/shard_map/cond/branch_1_fun/second_sums/pallas_call | solution.py:132
  24.7 0.1 collective-permute-start.2
  24.8 4.0 %collective-permute-done.3.cross = bf16[16,128,256]{2,1,0:T(8,128)(2,1)S(1)} collective-permute-done((bf16[16,128,256]{2,1,0:T(8,128)(2,1)}, bf16[16,128,256]{2,1,0:T(8,128)(2,1)S(1)}, u32[]{:S(2)}, u32[]{:S(2)}) %collective-permute-start.3) | collective-permute-done | bytes 1048608 | tf_op jit(solution)/shard_map/cond/branch_1_fun/ppermute | solution.py:204
  28.8 0.0 collective-permute-done.2.received
  28.8 0.4 partner_term.1
  29.2 0.0 collective-permute-done.4.straight
  29.2 1.2 %couple.1 = bf16[2,16,16,256]{3,2,1,0:T(8,128)(2,1)} custom-call(bf16[256,2048]{1,0:T(8,128)(2,1)S(1)} %get-tuple-element.28.mine, bf16[16,128,256]{2,1,0:T(8,128)(2,1)S(1)} %collective-permute-done.4.straight, f32[256,256]{1,0:T(8,128)S(1)} %get-tuple-element.29.part, bf16[16,16,256]{2,1,0:T(8,128)(2,1)S(1)} %get-tuple-element.30.own), custom_call_target="tpu_custom_call" | custom-call | flops 1000000000 | bytes 6291456 | tf_op jit(solution)/shard_map/couple/pallas_call | solution.py:173
  30.5 12.1 %all-to-all-start = ((bf16[32,16,256]{2,1,0:T(8,128)(2,1)}), bf16[32,16,256]{2,1,0:T(8,128)(2,1)S(1)}, u32[]{:S(2)}, u32[]{:S(2)}) async-start(bf16[32,16,256]{2,1,0:T(8,128)(2,1)} %bitcast), calls=%async_computation | async-start | bytes 524288 | tf_op jit(solution)/shard_map/all_to_all | solution.py:227
  42.6 7.4 %all-to-all-done = bf16[32,16,256]{2,1,0:T(8,128)(2,1)S(1)} async-done(((bf16[32,16,256]{2,1,0:T(8,128)(2,1)}), bf16[32,16,256]{2,1,0:T(8,128)(2,1)S(1)}, u32[]{:S(2)}, u32[]{:S(2)}) %all-to-all-start) | async-done | bytes 262176 | tf_op jit(solution)/shard_map/all_to_all | solution.py:227
  50.0 0.1 collective-permute-start.5
  50.2 1.2 %collective-permute-done.5 = f32[2,8,256]{2,1,0:T(8,128)S(1)} collective-permute-done((f32[2,8,256]{2,1,0:T(8,128)S(1)}, f32[2,8,256]{2,1,0:T(8,128)S(1)}, u32[]{:S(2)}, u32[]{:S(2)}) %collective-permute-start.5) | collective-permute-done | bytes 16416 | tf_op jit(solution)/shard_map/ppermute | solution.py:233
  51.3 0.6 %maximum_bitcast_fusion = f32[1,8,768]{2,1,0:T(8,128)} fusion(f32[8,256]{1,0:T(8,128)S(1)} %get-tuple-element.41, f32[8,256]{1,0:T(8,128)S(1)} %get-tuple-element.40, f32[8,256]{1,0:T(8,128)S(1)} %get-tuple-element.39), kind=kLoop, calls=%fused_computation.3 | loop fusion | flops 12288 | bytes 49152 | tf_op jit(solution)/shard_map/broadcast_in_dim | solution.py:238
  (5 shorter events, 0.1 us)
Async XLA Ops:
  0.0 29.2 %collective-permute-start.4 = (bf16[16,128,256]{2,1,0:T(8,128)(2,1)}, bf16[16,128,256]{2,1,0:T(8,128)(2,1)S(1)}, u32[]{:S(2)}, u32[]{:S(2)}) collective-permute-start(bf16[16,128,256]{2,1,0:T(8,128)(2,1)} %param.11), channel_id=1, source_target_pairs={{0,1},{2,3},{4,5},{6,7},{1,0},{3,2},{5,4},{7,6},{9,10},{11,12},{13... | collective-permute-start | bytes 3145736 | tf_op jit(solution)/shard_map/ppermute | solution.py:197
  0.7 12.2 %collective-permute-start.1 = (bf16[16,128,256]{2,1,0:T(8,128)(2,1)}, bf16[16,128,256]{2,1,0:T(8,128)(2,1)S(1)}, u32[]{:S(2)}, u32[]{:S(2)}) collective-permute-start(bf16[16,128,256]{2,1,0:T(8,128)(2,1)} %get-tuple-element.21.own), channel_id=1, source_target_pairs={{0,8},{16,24},{32,40},{48,56},{64,72},{80,88},{96,104},{112,120},{... | collective-permute-start | bytes 3145736 | tf_op jit(solution)/shard_map/cond/branch_1_fun/ppermute | solution.py:203
  5.4 16.6 %collective-permute-start = (bf16[16,128,256]{2,1,0:T(8,128)(2,1)}, bf16[16,128,256]{2,1,0:T(8,128)(2,1)S(1)}, u32[]{:S(2)}, u32[]{:S(2)}) collective-permute-start(bf16[16,128,256]{2,1,0:T(8,128)(2,1)} %get-tuple-element.21.own), channel_id=1, source_target_pairs={{8,16},{24,32},{40,48},{56,64},{72,80},{88,96},{104,112},{120,128}... | collective-permute-start | bytes 3145736 | tf_op jit(solution)/shard_map/cond/branch_1_fun/ppermute | solution.py:202
  8.5 20.3 %collective-permute-start.3 = (bf16[16,128,256]{2,1,0:T(8,128)(2,1)}, bf16[16,128,256]{2,1,0:T(8,128)(2,1)S(1)}, u32[]{:S(2)}, u32[]{:S(2)}) collective-permute-start(bf16[16,128,256]{2,1,0:T(8,128)(2,1)} %get-tuple-element.21.own), channel_id=1, source_target_pairs={{1,10},{3,12},{5,14},{2,9},{4,11},{6,13},{8,1},{10,3},{12,5},{14,7... | collective-permute-start | bytes 3145736 | tf_op jit(solution)/shard_map/cond/branch_1_fun/ppermute | solution.py:204
  9.8 3.4 %copy-start = (bf16[1,256,128,128]{3,2,1,0:T(8,128)(2,1)S(1)}, bf16[1,256,128,128]{3,2,1,0:T(8,128)(2,1)}, u32[]{:S(2)}) copy-start(bf16[1,256,128,128]{3,2,1,0:T(8,128)(2,1)} %get-tuple-element.38.a_tiles) | copy-start | bytes 25165828 | tf_op jit(solution)/shard_map/cond
  9.8 3.6 %copy-start.1 = (bf16[16,128,256]{2,1,0:T(8,128)(2,1)S(1)}, bf16[16,128,256]{2,1,0:T(8,128)(2,1)}, u32[]{:S(2)}) copy-start(bf16[16,128,256]{2,1,0:T(8,128)(2,1)} %get-tuple-element.21.own) | copy-start | bytes 3145732 | tf_op jit(solution)/shard_map/cond
  24.7 4.1 %collective-permute-start.2 = (bf16[256,2048]{1,0:T(8,128)(2,1)S(1)}, bf16[256,2048]{1,0:T(8,128)(2,1)S(1)}, u32[]{:S(2)}, u32[]{:S(2)}) collective-permute-start(bf16[256,2048]{1,0:T(8,128)(2,1)S(1)} %get-tuple-element.23), channel_id=1, source_target_pairs={{0,8},{16,24},{32,40},{48,56},{64,72},{80,88},{96,104},{112,120},{... | collective-permute-start | bytes 3145736 | tf_op jit(solution)/shard_map/cond/branch_1_fun/ppermute | solution.py:212
  30.5 19.5 %all-to-all-start = ((bf16[32,16,256]{2,1,0:T(8,128)(2,1)}), bf16[32,16,256]{2,1,0:T(8,128)(2,1)S(1)}, u32[]{:S(2)}, u32[]{:S(2)}) async-start(bf16[32,16,256]{2,1,0:T(8,128)(2,1)} %bitcast), calls=%async_computation | async-start | bytes 524288 | tf_op jit(solution)/shard_map/all_to_all | solution.py:227
  50.0 1.3 %collective-permute-start.5 = (f32[2,8,256]{2,1,0:T(8,128)S(1)}, f32[2,8,256]{2,1,0:T(8,128)S(1)}, u32[]{:S(2)}, u32[]{:S(2)}) collective-permute-start(f32[2,8,256]{2,1,0:T(8,128)S(1)} %get-tuple-element.42), channel_id=1, source_target_pairs={{0,8},{16,24},{32,40},{48,56},{64,72},{80,88},{96,104},{112,120},{... | collective-permute-start | bytes 49160 | tf_op jit(solution)/shard_map/ppermute | solution.py:233

commit v5 on v4

--- a/solution.py
+++ b/solution.py
@@ -104,16 +104,37 @@
     return term.T.reshape(TERMS).astype(BF)
 
 
-def second_kernel(
-    codes, counts, a_tiles, other, before, own, sums, mine, theirs, terms, turned
-):
-    core = lax.axis_index("row") & 1
-    apply_tiles(2 * core, codes, counts, a_tiles, other, sums)
-    offset = 2 * (1 - ((lax.axis_index("col") ^ core) & 1))
-    for part, ref in ((offset, mine), (2 - offset, theirs), (1, turned)):
-        for k in range(PANELS):
-            ref[:, pl.ds(k * TILE, TILE)] = sums[part * PANELS + k].astype(BF).T
+def turn(sums, part, ref):
+    for k in range(PANELS):
+        ref[:, pl.ds(k * TILE, TILE)] = sums[part * PANELS + k].astype(BF).T
+
+
+def my_offset():
+    return 2 * (1 - ((lax.axis_index("col") ^ lax.axis_index("row")) & 1))
+
+
+def second_kernel(codes, counts, a_tiles, other, before, sums, theirs):
+    apply_tiles(2 * (lax.axis_index("row") & 1), codes, counts, a_tiles, other, sums)
+    turn(sums, 2 - my_offset(), theirs)
+
+
+def own_kernel(sums, own, mine, terms, turned):
+    turn(sums, my_offset(), mine)
+    turn(sums, 1, turned)
     terms[...] = by_chip(term_of(turned, own))
+
+
+def own_terms(sums, own):
+    return pl.pallas_call(
+        own_kernel,
+        out_shape=(jax.ShapeDtypeStruct(TURNED, BF), jax.ShapeDtypeStruct(TERMS, BF)),
+        in_specs=[VM] * 2,
+        out_specs=(VM, VM),
+        scratch_shapes=[pltpu.VMEM(TURNED, BF)],
+        compiler_params=vmem(20),
+        name="own_terms",
+        cost_estimate=cost(10 * 10**9, 8 * 2**20),
+    )(sums, own)
 
 
 def first_sums(codes, counts, a_tiles, own, partner):
@@ -128,23 +149,17 @@
     )(codes, counts, a_tiles, own, partner)
 
 
-def second_sums(codes, counts, a_tiles, other, before, own):
+def second_sums(codes, counts, a_tiles, other, before):
     return pl.pallas_call(
         second_kernel,
-        out_shape=(
-            jax.ShapeDtypeStruct(SUMS, F32),
-            jax.ShapeDtypeStruct(TURNED, BF),
-            jax.ShapeDtypeStruct(TURNED, BF),
-            jax.ShapeDtypeStruct(TERMS, BF),
-        ),
-        in_specs=[SM] * 2 + [VM] * 4,
-        out_specs=(VM, VM, VM, VM),
-        scratch_shapes=[pltpu.VMEM(TURNED, BF)],
+        out_shape=(jax.ShapeDtypeStruct(SUMS, F32), jax.ShapeDtypeStruct(TURNED, BF)),
+        in_specs=[SM] * 2 + [VM] * 3,
+        out_specs=(VM, VM),
         input_output_aliases={4: 0},
         compiler_params=vmem(24),
         name="second_sums",
         cost_estimate=cost(10 * 10**9, 16 * 2**20),
-    )(codes, counts, a_tiles, other, before, own)[1:]
+    )(codes, counts, a_tiles, other, before)
 
 
 def partner_kernel(received, cross, part):
@@ -165,14 +180,14 @@
 
 def couple_kernel(mine, straight, part, own, out):
     upper_band = (lax.axis_index("row") ^ lax.axis_index("col")) & 1
-    out[upper_band] = own[...]
-    out[1 - upper_band] = by_chip(term_of(mine, straight) + part[...])
+    out[:, upper_band] = own[...]
+    out[:, 1 - upper_band] = by_chip(term_of(mine, straight) + part[...])
 
 
 def couple(mine, straight, part, own):
     return pl.pallas_call(
         couple_kernel,
-        out_shape=jax.ShapeDtypeStruct((2,) + TERMS, BF),
+        out_shape=jax.ShapeDtypeStruct((CHIPS, 2) + TERMS[1:], BF),
         in_specs=[VM] * 4,
         out_specs=VM,
         compiler_params=vmem(8),
@@ -208,8 +223,10 @@
         ])
         codes, counts = plan(a_rows, a_cols, a_count)
         before = first_sums(codes, counts, a_tiles, p_panels, partner)
-        mine, theirs, terms = second_sums(codes, counts, a_tiles, other, before, p_panels)
-        return mine, partner_term(lax.ppermute(theirs, "row", chip), cross), terms
+        after, theirs = second_sums(codes, counts, a_tiles, other, before)
+        received = lax.ppermute(theirs, "row", chip)
+        mine, terms = own_terms(after, p_panels)
+        return mine, partner_term(received, cross), terms
 
     def nothing(_):
         return jnp.zeros(TURNED, BF), jnp.zeros((BAND, BAND), F32), jnp.zeros(TERMS, BF)
@@ -219,13 +236,13 @@
     first_core = (row & 1) == 0
     upper_band = ((row ^ col) & 1) == 1
     groups = [
-        [(2 * i + core) * n_col + (c + k) % n_col for k in range(2) for i in range(CHIPS)]
+        [(2 * i + core) * n_col + (c + k) % n_col for i in range(CHIPS) for k in range(2)]
         for core in range(2)
         for c in range(core, n_col, 2)
     ]
     both = both.reshape((2 * CHIPS,) + TERMS[1:])
     both = lax.all_to_all(both, ("row", "col"), 0, 0, axis_index_groups=groups)
-    lower, upper = both.reshape((2,) + TERMS).astype(F32).sum(1)
+    lower, upper = both.reshape((CHIPS, 2) + TERMS[1:]).astype(F32).sum(0)
     own = jnp.where(upper_band, upper, lower)
     ends = jnp.where(upper_band, lower, upper)
     mine = jnp.stack([own, ends]).reshape(2, 2, 8, BAND)

time: 52.5 us -> 51.7 us (0.985)
  starting transfers between devices: 22.1 us -> 21.5 us
    pallas_call x1 -> x2, Pallas kernels: 1.22 us -> 2.07 us  [the longest x1 1.21 us: couple(): pl.pallas_call(couple_kernel, out_shape=jax.ShapeDtypeStruct((CHIPS, 2) +...]
    pallas_call x1, Pallas kernels: 2.64 us -> 1.91 us  [second_sums(): pl.pallas_call(second_kernel, out_shape=(jax.ShapeDtypeStruct(SUMS, F32),...]
    all_to_all x1, starting transfers between devices: 12.1 us -> 11.5 us  [local(): both = lax.all_to_all(both, ('row', 'col'), 0, 0, axis_index_groups=groups)]
  transfers between devices with their start and end apart: 7 -> 7, of which waited for: 4 -> 4; matrix products, arithmetic and copies ran while one was open for 0% -> 0% of each run, Pallas kernels for 17% -> 18%
where the time goes in v5:
time: 51.7 us; the launch traced here: 51.4 us
  starting transfers between devices  21.5 us (42%)
  waiting for transfers between devices  18.1 us (35%)
  Pallas kernels  10.4 us (20%)
  other arithmetic  0.68 us (1%)
  local copies, waits for them, and re-layouts  0.55 us (1%)
    all_to_all x1, starting transfers between devices, local(): both = lax.all_to_all(both, ('row', 'col'), 0, 0, axis_index_groups=groups)  11.5 us
    all_to_all x1, waiting for transfers between devices, local(): both = lax.all_to_all(both, ('row', 'col'), 0, 0, axis_index_groups=groups)  7.46 us
    ppermute x1, waiting for transfers between devices, sums(): other = lax.ppermute(p_panels, 'row', bridges)  5.64 us
    ppermute x1, starting transfers between devices, sums(): partner = lax.ppermute(p_panels, 'row', chip)  4.69 us
    ppermute x1, waiting for transfers between devices, sums(): lax.ppermute(p_panels, ('row', 'col'), [(r * n_col + i, (r ^ 1) * n_col +...  3.86 us
    pallas_call x1, Pallas kernels, plan(): pl.pallas_call(plan_kernel, out_shape=(jax.ShapeDtypeStruct((3 * LIST + 1...  3.04 us
    ppermute x1, starting transfers between devices, sums(): other = lax.ppermute(p_panels, 'row', bridges)  3.02 us
    pallas_call x1, Pallas kernels, first_sums(): pl.pallas_call(first_kernel, out_shape=jax.ShapeDtypeStruct(SUMS, F32), i...  2.95 us
  transfers between devices with their start and end apart: 7, of which 4 were waited for; matrix products, arithmetic and copies ran while one was open for 0% of the time, Pallas kernels for 18%

profile of v5, /device:TPU:1, one launch (start us, length us, event | category | flops | bytes accessed | tf_op | source)
XLA Modules:
  0.0 51.4 jit_solution(1452743427908195766)
XLA Ops:
  0.0 0.7 %collective-permute-start.4 = (bf16[16,128,256]{2,1,0:T(8,128)(2,1)}, bf16[16,128,256]{2,1,0:T(8,128)(2,1)S(1)}, u32[]{:S(2)}, u32[]{:S(2)}) collective-permute-start(bf16[16,128,256]{2,1,0:T(8,128)(2,1)} %param.11), channel_id=1, source_target_pairs={{0,1},{2,3},{4,5},{6,7},{1,0},{3,2},{5,4},{7,6},{9,10},{11,12},{13... | collective-permute-start | bytes 3145736 | tf_op jit(solution)/shard_map/ppermute | solution.py:212
  0.7 28.5 %conditional.1 = (bf16[256,2048]{1,0:T(8,128)(2,1)S(1)}, f32[256,256]{1,0:T(8,128)S(1)}, bf16[16,16,256]{2,1,0:T(8,128)(2,1)S(1)}) conditional(s32[]{:T(128)} %convert_element_type.9, () %tuple.13, (s32[1,256]{1,0:T(1,128)}, s32[1,256]{1,0:T(1,128)}, s32[1,1]{1,0:T(1,128)}, bf16[16,128,256]{2,1,0:T(8,128)(2,1)}, ...), branch_computations={%region_0.0_spmd, %region_1.0_spmd} | conditional | flops 60999999488 | bytes 102770688 | solution.py:234
  0.7 4.7 %collective-permute-start.1 = (bf16[16,128,256]{2,1,0:T(8,128)(2,1)}, bf16[16,128,256]{2,1,0:T(8,128)(2,1)S(1)}, u32[]{:S(2)}, u32[]{:S(2)}) collective-permute-start(bf16[16,128,256]{2,1,0:T(8,128)(2,1)} %get-tuple-element.21.own), channel_id=1, source_target_pairs={{0,8},{16,24},{32,40},{48,56},{64,72},{80,88},{96,104},{112,120},{... | collective-permute-start | bytes 3145736 | tf_op jit(solution)/shard_map/cond/branch_1_fun/ppermute | solution.py:218
  5.4 3.0 %collective-permute-start = (bf16[16,128,256]{2,1,0:T(8,128)(2,1)}, bf16[16,128,256]{2,1,0:T(8,128)(2,1)S(1)}, u32[]{:S(2)}, u32[]{:S(2)}) collective-permute-start(bf16[16,128,256]{2,1,0:T(8,128)(2,1)} %get-tuple-element.21.own), channel_id=1, source_target_pairs={{8,16},{24,32},{40,48},{56,64},{72,80},{88,96},{104,112},{120,128}... | collective-permute-start | bytes 3145736 | tf_op jit(solution)/shard_map/cond/branch_1_fun/ppermute | solution.py:217
  8.5 1.4 %collective-permute-start.3 = (bf16[16,128,256]{2,1,0:T(8,128)(2,1)}, bf16[16,128,256]{2,1,0:T(8,128)(2,1)S(1)}, u32[]{:S(2)}, u32[]{:S(2)}) collective-permute-start(bf16[16,128,256]{2,1,0:T(8,128)(2,1)} %get-tuple-element.21.own), channel_id=1, source_target_pairs={{1,10},{3,12},{5,14},{2,9},{4,11},{6,13},{8,1},{10,3},{12,5},{14,7... | collective-permute-start | bytes 3145736 | tf_op jit(solution)/shard_map/cond/branch_1_fun/ppermute | solution.py:219
  9.8 3.0 %plan.1 = (s32[817]{0:T(1024)S(1)}, s32[3]{0:T(128)S(1)}) custom-call(s32[1,256]{1,0:T(1,128)} %get-tuple-element.36.rows, s32[1,256]{1,0:T(1,128)} %get-tuple-element.37.cols, s32[1,1]{1,0:T(1,128)} %get-tuple-element.38.count), custom_call_target="tpu_custom_call" | custom-call | flops 30000001024 | bytes 10000 | tf_op jit(solution)/shard_map/cond/branch_1_fun/plan/pallas_call | solution.py:59
  12.9 0.0 collective-permute-done.1.partner
  12.9 0.3 copy-done
  13.2 0.2 copy-done.1
  13.4 3.0 %first_sums.1.before = f32[49,128,256]{2,1,0:T(8,128)S(1)} custom-call(s32[817]{0:T(1024)S(1)} %get-tuple-element.18.codes, s32[3]{0:T(128)S(1)} %get-tuple-element.19.counts, bf16[1,256,128,128]{3,2,1,0:T(8,128)(2,1)S(1)} %copy-done, bf16[16,128,256]{2,1,0:T(8,128)(2,1)S(1)} %copy-done.1, bf16[16,128,256]{2,1,0:T(8,128)(2,1)S(1)} %collective-permute-done.1.partner), custom_call_target="tpu_custom_call" | custom-call | flops 10000000000 | bytes 16777216 | tf_op jit(solution)/shard_map/cond/branch_1_fun/first_sums/pallas_call | solution.py:141
  16.4 5.6 %collective-permute-done.other = bf16[16,128,256]{2,1,0:T(8,128)(2,1)S(1)} collective-permute-done((bf16[16,128,256]{2,1,0:T(8,128)(2,1)}, bf16[16,128,256]{2,1,0:T(8,128)(2,1)S(1)}, u32[]{:S(2)}, u32[]{:S(2)}) %collective-permute-start) | collective-permute-done | bytes 1048608 | tf_op jit(solution)/shard_map/cond/branch_1_fun/ppermute | solution.py:217
  22.0 1.9 %second_sums.1 = (f32[49,128,256]{2,1,0:T(8,128)S(1)}, bf16[256,2048]{1,0:T(8,128)(2,1)S(1)}) custom-call(s32[817]{0:T(1024)S(1)} %get-tuple-element.18.codes, s32[3]{0:T(128)S(1)} %get-tuple-element.19.counts, bf16[1,256,128,128]{3,2,1,0:T(8,128)(2,1)S(1)} %copy-done, ...), custom_call_target="tpu_custom_call", output_to_operand_aliasing={{0}: (4, {})} | custom-call | flops 10000000000 | bytes 16777216 | tf_op jit(solution)/shard_map/cond/branch_1_fun/second_sums/pallas_call | solution.py:153
  24.0 0.1 collective-permute-start.2
  24.1 0.9 %own_terms.1 = (bf16[256,2048]{1,0:T(8,128)(2,1)S(1)}, bf16[16,16,256]{2,1,0:T(8,128)(2,1)S(1)}) custom-call(f32[49,128,256]{2,1,0:T(8,128)S(1)} %get-tuple-element.22.sums, bf16[16,128,256]{2,1,0:T(8,128)(2,1)S(1)} %copy-done.1), custom_call_target="tpu_custom_call" | custom-call | flops 10000000000 | bytes 8388608 | tf_op jit(solution)/shard_map/cond/branch_1_fun/own_terms/pallas_call | solution.py:128
  24.9 3.9 %collective-permute-done.3.cross = bf16[16,128,256]{2,1,0:T(8,128)(2,1)S(1)} collective-permute-done((bf16[16,128,256]{2,1,0:T(8,128)(2,1)}, bf16[16,128,256]{2,1,0:T(8,128)(2,1)S(1)}, u32[]{:S(2)}, u32[]{:S(2)}) %collective-permute-start.3) | collective-permute-done | bytes 1048608 | tf_op jit(solution)/shard_map/cond/branch_1_fun/ppermute | solution.py:219
  28.8 0.0 collective-permute-done.2.received
  28.8 0.4 partner_term.1
  29.2 0.0 collective-permute-done.4.straight
  29.2 1.2 %couple.1 = bf16[16,2,16,256]{3,2,1,0:T(8,128)(2,1)} custom-call(bf16[256,2048]{1,0:T(8,128)(2,1)S(1)} %get-tuple-element.29.mine, bf16[16,128,256]{2,1,0:T(8,128)(2,1)S(1)} %collective-permute-done.4.straight, f32[256,256]{1,0:T(8,128)S(1)} %get-tuple-element.30.part, bf16[16,16,256]{2,1,0:T(8,128)(2,1)S(1)} %get-tuple-element.31.own), custom_call_target="tpu_custom_call" | custom-call | flops 1000000000 | bytes 6291456 | tf_op jit(solution)/shard_map/couple/pallas_call | solution.py:188
  30.5 11.5 %all-to-all-start = ((bf16[32,16,256]{2,1,0:T(8,128)(2,1)}), bf16[32,16,256]{2,1,0:T(8,128)(2,1)S(1)}, u32[]{:S(2)}, u32[]{:S(2)}) async-start(bf16[32,16,256]{2,1,0:T(8,128)(2,1)} %bitcast), calls=%async_computation | async-start | bytes 524288 | tf_op jit(solution)/shard_map/all_to_all | solution.py:244
  41.9 7.5 %all-to-all-done = bf16[32,16,256]{2,1,0:T(8,128)(2,1)S(1)} async-done(((bf16[32,16,256]{2,1,0:T(8,128)(2,1)}), bf16[32,16,256]{2,1,0:T(8,128)(2,1)S(1)}, u32[]{:S(2)}, u32[]{:S(2)}) %all-to-all-start) | async-done | bytes 262176 | tf_op jit(solution)/shard_map/all_to_all | solution.py:244
  49.5 0.1 collective-permute-start.5
  49.6 1.1 %collective-permute-done.5 = f32[2,8,256]{2,1,0:T(8,128)S(1)} collective-permute-done((f32[2,8,256]{2,1,0:T(8,128)S(1)}, f32[2,8,256]{2,1,0:T(8,128)S(1)}, u32[]{:S(2)}, u32[]{:S(2)}) %collective-permute-start.5) | collective-permute-done | bytes 16416 | tf_op jit(solution)/shard_map/ppermute | solution.py:250
  50.7 0.6 %maximum_bitcast_fusion = f32[1,8,768]{2,1,0:T(8,128)} fusion(f32[8,256]{1,0:T(8,128)S(1)} %get-tuple-element.42, f32[8,256]{1,0:T(8,128)S(1)} %get-tuple-element.41, f32[8,256]{1,0:T(8,128)S(1)} %get-tuple-element.40), kind=kLoop, calls=%fused_computation.3 | loop fusion | flops 12288 | bytes 49152 | tf_op jit(solution)/shard_map/broadcast_in_dim | solution.py:255
  (6 shorter events, 0.1 us)
Async XLA Ops:
  0.0 29.2 %collective-permute-start.4 = (bf16[16,128,256]{2,1,0:T(8,128)(2,1)}, bf16[16,128,256]{2,1,0:T(8,128)(2,1)S(1)}, u32[]{:S(2)}, u32[]{:S(2)}) collective-permute-start(bf16[16,128,256]{2,1,0:T(8,128)(2,1)} %param.11), channel_id=1, source_target_pairs={{0,1},{2,3},{4,5},{6,7},{1,0},{3,2},{5,4},{7,6},{9,10},{11,12},{13... | collective-permute-start | bytes 3145736 | tf_op jit(solution)/shard_map/ppermute | solution.py:212
  0.7 12.2 %collective-permute-start.1 = (bf16[16,128,256]{2,1,0:T(8,128)(2,1)}, bf16[16,128,256]{2,1,0:T(8,128)(2,1)S(1)}, u32[]{:S(2)}, u32[]{:S(2)}) collective-permute-start(bf16[16,128,256]{2,1,0:T(8,128)(2,1)} %get-tuple-element.21.own), channel_id=1, source_target_pairs={{0,8},{16,24},{32,40},{48,56},{64,72},{80,88},{96,104},{112,120},{... | collective-permute-start | bytes 3145736 | tf_op jit(solution)/shard_map/cond/branch_1_fun/ppermute | solution.py:218
  5.4 16.6 %collective-permute-start = (bf16[16,128,256]{2,1,0:T(8,128)(2,1)}, bf16[16,128,256]{2,1,0:T(8,128)(2,1)S(1)}, u32[]{:S(2)}, u32[]{:S(2)}) collective-permute-start(bf16[16,128,256]{2,1,0:T(8,128)(2,1)} %get-tuple-element.21.own), channel_id=1, source_target_pairs={{8,16},{24,32},{40,48},{56,64},{72,80},{88,96},{104,112},{120,128}... | collective-permute-start | bytes 3145736 | tf_op jit(solution)/shard_map/cond/branch_1_fun/ppermute | solution.py:217
  8.5 20.3 %collective-permute-start.3 = (bf16[16,128,256]{2,1,0:T(8,128)(2,1)}, bf16[16,128,256]{2,1,0:T(8,128)(2,1)S(1)}, u32[]{:S(2)}, u32[]{:S(2)}) collective-permute-start(bf16[16,128,256]{2,1,0:T(8,128)(2,1)} %get-tuple-element.21.own), channel_id=1, source_target_pairs={{1,10},{3,12},{5,14},{2,9},{4,11},{6,13},{8,1},{10,3},{12,5},{14,7... | collective-permute-start | bytes 3145736 | tf_op jit(solution)/shard_map/cond/branch_1_fun/ppermute | solution.py:219
  9.8 3.4 %copy-start = (bf16[1,256,128,128]{3,2,1,0:T(8,128)(2,1)S(1)}, bf16[1,256,128,128]{3,2,1,0:T(8,128)(2,1)}, u32[]{:S(2)}) copy-start(bf16[1,256,128,128]{3,2,1,0:T(8,128)(2,1)} %get-tuple-element.39.a_tiles) | copy-start | bytes 25165828 | tf_op jit(solution)/shard_map/cond
  9.8 3.6 %copy-start.1 = (bf16[16,128,256]{2,1,0:T(8,128)(2,1)S(1)}, bf16[16,128,256]{2,1,0:T(8,128)(2,1)}, u32[]{:S(2)}) copy-start(bf16[16,128,256]{2,1,0:T(8,128)(2,1)} %get-tuple-element.21.own) | copy-start | bytes 3145732 | tf_op jit(solution)/shard_map/cond
  24.0 4.8 %collective-permute-start.2 = (bf16[256,2048]{1,0:T(8,128)(2,1)S(1)}, bf16[256,2048]{1,0:T(8,128)(2,1)S(1)}, u32[]{:S(2)}, u32[]{:S(2)}) collective-permute-start(bf16[256,2048]{1,0:T(8,128)(2,1)S(1)} %get-tuple-element.24), channel_id=1, source_target_pairs={{0,8},{16,24},{32,40},{48,56},{64,72},{80,88},{96,104},{112,120},{... | collective-permute-start | bytes 3145736 | tf_op jit(solution)/shard_map/cond/branch_1_fun/ppermute | solution.py:227
  30.5 18.9 %all-to-all-start = ((bf16[32,16,256]{2,1,0:T(8,128)(2,1)}), bf16[32,16,256]{2,1,0:T(8,128)(2,1)S(1)}, u32[]{:S(2)}, u32[]{:S(2)}) async-start(bf16[32,16,256]{2,1,0:T(8,128)(2,1)} %bitcast), calls=%async_computation | async-start | bytes 524288 | tf_op jit(solution)/shard_map/all_to_all | solution.py:244
  49.5 1.3 %collective-permute-start.5 = (f32[2,8,256]{2,1,0:T(8,128)S(1)}, f32[2,8,256]{2,1,0:T(8,128)S(1)}, u32[]{:S(2)}, u32[]{:S(2)}) collective-permute-start(f32[2,8,256]{2,1,0:T(8,128)S(1)} %get-tuple-element.43), channel_id=1, source_target_pairs={{0,8},{16,24},{32,40},{48,56},{64,72},{80,88},{96,104},{112,120},{... | collective-permute-start | bytes 49160 | tf_op jit(solution)/shard_map/ppermute | solution.py:250

commit v6 on v5

--- a/solution.py
+++ b/solution.py
@@ -196,18 +196,62 @@
     )(mine, straight, part, own)
 
 
+def fold_kernel(both, kept, given):
+    core = lax.axis_index("row") & 1
+    upper_band = core ^ (lax.axis_index("col") & 1)
+    for at, band in ((0, upper_band), (1, 1 - upper_band)):
+        total = both[0, band].astype(F32)
+        for i in range(1, CHIPS):
+            total = total + both[i, band].astype(F32)
+        first = core == 0
+        kept[at] = jnp.where(first, total[:8], total[8:])
+        given[at] = jnp.where(first, total[8:], total[:8])
+
+
+def fold(both):
+    half = jax.ShapeDtypeStruct((2, 8, BAND), F32)
+    return pl.pallas_call(
+        fold_kernel,
+        out_shape=(half, half),
+        in_specs=[VM],
+        out_specs=(VM, VM),
+        compiler_params=vmem(4),
+        name="fold",
+        cost_estimate=cost(10**5, 10**5),
+    )(both)
+
+
+def finish_kernel(kept, given, out):
+    core, col = lax.axis_index("row") & 1, lax.axis_index("col") & 1
+    kept_is_upper = core == col
+    out[:, :BAND] = jnp.where(kept_is_upper, given[1], kept[1])
+    out[:, BAND:2 * BAND] = kept[0] + given[0]
+    out[:, 2 * BAND:] = jnp.where(kept_is_upper, kept[1], given[1])
+
+
+def finish(kept, given):
+    return pl.pallas_call(
+        finish_kernel,
+        out_shape=jax.ShapeDtypeStruct((8, 3 * BAND), F32),
+        in_specs=[VM, VM],
+        out_specs=VM,
+        compiler_params=vmem(4),
+        name="finish",
+        cost_estimate=cost(10**4, 10**5),
+    )(kept, given)
+
+
 def both_ways(pairs):
     return pairs + [(j, i) for i, j in pairs]
 
 
 def local(a_tiles, a_rows, a_cols, a_count, p_panels):
     n_row, n_col = lax.axis_size("row"), lax.axis_size("col")
-    row, col = lax.axis_index("row"), lax.axis_index("col")
+    row = lax.axis_index("row")
     even_pairs = both_ways([(i, i + 1) for i in range(0, n_col - 1, 2)])
     odd_pairs = both_ways([(i, i + 1) for i in range(1, n_col - 1, 2)])
     chip = both_ways([(i, i + 1) for i in range(0, n_row - 1, 2)])
     bridges = both_ways([(i, i + 1) for i in range(1, n_row - 1, 2)])
-    low_col = (col & 1) == 0
     col_pairs = (even_pairs, odd_pairs)
     straight = lax.ppermute(p_panels, ("row", "col"), [
         (r * n_col + i, r * n_col + j) for r in range(n_row) for i, j in col_pairs[r & 1]
@@ -233,8 +277,6 @@
 
     mine, part, terms = lax.cond(row < n_row, sums, nothing, 0)
     both = couple(mine, straight, part, terms)
-    first_core = (row & 1) == 0
-    upper_band = ((row ^ col) & 1) == 1
     groups = [
         [(2 * i + core) * n_col + (c + k) % n_col for i in range(CHIPS) for k in range(2)]
         for core in range(2)
@@ -242,17 +284,8 @@
     ]
     both = both.reshape((2 * CHIPS,) + TERMS[1:])
     both = lax.all_to_all(both, ("row", "col"), 0, 0, axis_index_groups=groups)
-    lower, upper = both.reshape((CHIPS, 2) + TERMS[1:]).astype(F32).sum(0)
-    own = jnp.where(upper_band, upper, lower)
-    ends = jnp.where(upper_band, lower, upper)
-    mine = jnp.stack([own, ends]).reshape(2, 2, 8, BAND)
-    kept = jnp.where(first_core, mine[:, 0], mine[:, 1])
-    given = lax.ppermute(jnp.where(first_core, mine[:, 1], mine[:, 0]), "row", chip)
-    from_even = jnp.where(first_core, kept[1], given[1])
-    from_odd = jnp.where(first_core, given[1], kept[1])
-    left = jnp.where(low_col, from_odd, from_even)
-    right = jnp.where(low_col, from_even, from_odd)
-    return jnp.concatenate([left, kept[0] + given[0], right], axis=1)[None]
+    mine, given = fold(both.reshape((CHIPS, 2) + TERMS[1:]))
+    return finish(mine, lax.ppermute(given, "row", chip))[None]
 
 
 def solution(mesh):

time: 51.7 us -> 50.7 us (0.981)
  blocking collectives: 0 us -> 18.7 us
  starting transfers between devices: 21.5 us -> 10 us
  waiting for transfers between devices: 18.1 us -> 9.49 us
  Pallas kernels: 10.4 us -> 12 us
  other arithmetic: 0.68 us -> 0 us
    all_to_all x0 -> x1, blocking collectives: none -> 18.7 us  [local(): both = lax.all_to_all(both, ('row', 'col'), 0, 0, axis_index_groups=groups)]
    all_to_all x1 -> x0, starting transfers between devices: 11.5 us -> none  [local(): both = lax.all_to_all(both, ('row', 'col'), 0, 0, axis_index_groups=groups)]
    all_to_all x1 -> x0, waiting for transfers between devices: 7.46 us -> none  [local(): both = lax.all_to_all(both, ('row', 'col'), 0, 0, axis_index_groups=groups)]
    ppermute x1, waiting for transfers between devices: 5.64 us -> 4.84 us  [sums(): other = lax.ppermute(p_panels, 'row', bridges)]
    pallas_call x1, Pallas kernels: 2.95 us -> 3.74 us  [first_sums(): pl.pallas_call(first_kernel, out_shape=jax.ShapeDtypeStruct(SUMS, F32), i...]
    pallas_call x1, Pallas kernels: 1.21 us -> 0.51 us  [couple(): pl.pallas_call(couple_kernel, out_shape=jax.ShapeDtypeStruct((CHIPS, 2) +...]
    pallas_call x0 -> x2, Pallas kernels: none -> 0.65 us  [the longest x1 0.61 us: finish(): pl.pallas_call(finish_kernel, out_shape=jax.ShapeDtypeStruct((8, 3 * BAND...]
    broadcast_in_dim x1 -> x0, other arithmetic: 0.61 us -> none  [local(): return jnp.concatenate([left, kept[0] + given[0], right], axis=1)[None]]
  transfers between devices with their start and end apart: 7 -> 6, of which waited for: 4 -> 3; matrix products, arithmetic and copies ran while one was open for 0% -> 0% of each run, Pallas kernels for 18% -> 21%
where the time goes in v6:
time: 50.7 us; the launch traced here: 50.4 us
  blocking collectives  18.7 us (37%)
  Pallas kernels  12 us (24%)
  starting transfers between devices  10 us (20%)
  waiting for transfers between devices  9.49 us (19%)
    all_to_all x1, blocking collectives, local(): both = lax.all_to_all(both, ('row', 'col'), 0, 0, axis_index_groups=groups)  18.7 us
    ppermute x1, waiting for transfers between devices, sums(): other = lax.ppermute(p_panels, 'row', bridges)  4.84 us
    ppermute x1, starting transfers between devices, sums(): partner = lax.ppermute(p_panels, 'row', chip)  4.69 us
    pallas_call x1, Pallas kernels, first_sums(): pl.pallas_call(first_kernel, out_shape=jax.ShapeDtypeStruct(SUMS, F32), i...  3.74 us
    ppermute x1, waiting for transfers between devices, sums(): lax.ppermute(p_panels, ('row', 'col'), [(r * n_col + i, (r ^ 1) * n_col +...  3.49 us
    pallas_call x1, Pallas kernels, plan(): pl.pallas_call(plan_kernel, out_shape=(jax.ShapeDtypeStruct((3 * LIST + 1...  3.48 us
    ppermute x1, starting transfers between devices, sums(): other = lax.ppermute(p_panels, 'row', bridges)  3.02 us
    pallas_call x1, Pallas kernels, second_sums(): pl.pallas_call(second_kernel, out_shape=(jax.ShapeDtypeStruct(SUMS, F32),...  2.31 us
  transfers between devices with their start and end apart: 6, of which 3 were waited for; matrix products, arithmetic and copies ran while one was open for 0% of the time, Pallas kernels for 21%

profile of v6, /device:TPU:1, one launch (start us, length us, event | category | flops | bytes accessed | tf_op | source)
XLA Modules:
  0.0 50.4 jit_solution(14811043507707520803)
XLA Ops:
  0.0 0.7 %collective-permute-start.4 = (bf16[16,128,256]{2,1,0:T(8,128)(2,1)}, bf16[16,128,256]{2,1,0:T(8,128)(2,1)S(1)}, u32[]{:S(2)}, u32[]{:S(2)}) collective-permute-start(bf16[16,128,256]{2,1,0:T(8,128)(2,1)} %param.11), channel_id=1, source_target_pairs={{0,1},{2,3},{4,5},{6,7},{1,0},{3,2},{5,4},{7,6},{9,10},{11,12},{13... | collective-permute-start | bytes 3145736 | tf_op jit(solution)/shard_map/ppermute | solution.py:256
  0.7 28.5 %conditional.1 = (bf16[256,2048]{1,0:T(8,128)(2,1)S(1)}, f32[256,256]{1,0:T(8,128)S(1)}, bf16[16,16,256]{2,1,0:T(8,128)(2,1)S(1)}) conditional(s32[]{:T(128)} %convert_element_type.3, () %tuple.13, (s32[1,256]{1,0:T(1,128)}, s32[1,256]{1,0:T(1,128)}, s32[1,1]{1,0:T(1,128)}, bf16[16,128,256]{2,1,0:T(8,128)(2,1)}, ...), branch_computations={%region_0.0_spmd, %region_1.0_spmd} | conditional | flops 60999999488 | bytes 102770688 | solution.py:278
  0.7 4.7 %collective-permute-start.1 = (bf16[16,128,256]{2,1,0:T(8,128)(2,1)}, bf16[16,128,256]{2,1,0:T(8,128)(2,1)S(1)}, u32[]{:S(2)}, u32[]{:S(2)}) collective-permute-start(bf16[16,128,256]{2,1,0:T(8,128)(2,1)} %get-tuple-element.21.own), channel_id=1, source_target_pairs={{0,8},{16,24},{32,40},{48,56},{64,72},{80,88},{96,104},{112,120},{... | collective-permute-start | bytes 3145736 | tf_op jit(solution)/shard_map/cond/branch_1_fun/ppermute | solution.py:262
  5.4 3.0 %collective-permute-start = (bf16[16,128,256]{2,1,0:T(8,128)(2,1)}, bf16[16,128,256]{2,1,0:T(8,128)(2,1)S(1)}, u32[]{:S(2)}, u32[]{:S(2)}) collective-permute-start(bf16[16,128,256]{2,1,0:T(8,128)(2,1)} %get-tuple-element.21.own), channel_id=1, source_target_pairs={{8,16},{24,32},{40,48},{56,64},{72,80},{88,96},{104,112},{120,128}... | collective-permute-start | bytes 3145736 | tf_op jit(solution)/shard_map/cond/branch_1_fun/ppermute | solution.py:261
  8.4 1.4 %collective-permute-start.3 = (bf16[16,128,256]{2,1,0:T(8,128)(2,1)}, bf16[16,128,256]{2,1,0:T(8,128)(2,1)S(1)}, u32[]{:S(2)}, u32[]{:S(2)}) collective-permute-start(bf16[16,128,256]{2,1,0:T(8,128)(2,1)} %get-tuple-element.21.own), channel_id=1, source_target_pairs={{1,10},{3,12},{5,14},{2,9},{4,11},{6,13},{8,1},{10,3},{12,5},{14,7... | collective-permute-start | bytes 3145736 | tf_op jit(solution)/shard_map/cond/branch_1_fun/ppermute | solution.py:263
  9.8 0.0 copy-start
  9.8 0.0 copy-start.1
  9.8 3.5 %plan.1 = (s32[817]{0:T(1024)S(1)}, s32[3]{0:T(128)S(1)}) custom-call(s32[1,256]{1,0:T(1,128)} %get-tuple-element.40.rows, s32[1,256]{1,0:T(1,128)} %get-tuple-element.41.cols, s32[1,1]{1,0:T(1,128)} %get-tuple-element.42.count), custom_call_target="tpu_custom_call" | custom-call | flops 30000001024 | bytes 10000 | tf_op jit(solution)/shard_map/cond/branch_1_fun/plan/pallas_call | solution.py:59
  13.3 0.0 collective-permute-done.1.partner
  13.3 0.1 copy-done.1
  13.4 3.7 %first_sums.1.before = f32[49,128,256]{2,1,0:T(8,128)S(1)} custom-call(s32[817]{0:T(1024)S(1)} %get-tuple-element.18.codes, s32[3]{0:T(128)S(1)} %get-tuple-element.19.counts, bf16[1,256,128,128]{3,2,1,0:T(8,128)(2,1)S(1)} %copy-done, bf16[16,128,256]{2,1,0:T(8,128)(2,1)S(1)} %copy-done.1, bf16[16,128,256]{2,1,0:T(8,128)(2,1)S(1)} %collective-permute-done.1.partner), custom_call_target="tpu_custom_call" | custom-call | flops 10000000000 | bytes 16777216 | tf_op jit(solution)/shard_map/cond/branch_1_fun/first_sums/pallas_call | solution.py:141
  17.2 4.8 %collective-permute-done.other = bf16[16,128,256]{2,1,0:T(8,128)(2,1)S(1)} collective-permute-done((bf16[16,128,256]{2,1,0:T(8,128)(2,1)}, bf16[16,128,256]{2,1,0:T(8,128)(2,1)S(1)}, u32[]{:S(2)}, u32[]{:S(2)}) %collective-permute-start) | collective-permute-done | bytes 1048608 | tf_op jit(solution)/shard_map/cond/branch_1_fun/ppermute | solution.py:261
  22.0 2.3 %second_sums.1 = (f32[49,128,256]{2,1,0:T(8,128)S(1)}, bf16[256,2048]{1,0:T(8,128)(2,1)S(1)}) custom-call(s32[817]{0:T(1024)S(1)} %get-tuple-element.18.codes, s32[3]{0:T(128)S(1)} %get-tuple-element.19.counts, bf16[1,256,128,128]{3,2,1,0:T(8,128)(2,1)S(1)} %copy-done, ...), custom_call_target="tpu_custom_call", output_to_operand_aliasing={{0}: (4, {})} | custom-call | flops 10000000000 | bytes 16777216 | tf_op jit(solution)/shard_map/cond/branch_1_fun/second_sums/pallas_call | solution.py:153
  24.3 0.1 collective-permute-start.2
  24.4 0.8 %own_terms.1 = (bf16[256,2048]{1,0:T(8,128)(2,1)S(1)}, bf16[16,16,256]{2,1,0:T(8,128)(2,1)S(1)}) custom-call(f32[49,128,256]{2,1,0:T(8,128)S(1)} %get-tuple-element.22.sums, bf16[16,128,256]{2,1,0:T(8,128)(2,1)S(1)} %copy-done.1), custom_call_target="tpu_custom_call" | custom-call | flops 10000000000 | bytes 8388608 | tf_op jit(solution)/shard_map/cond/branch_1_fun/own_terms/pallas_call | solution.py:128
  25.3 3.5 %collective-permute-done.3.cross = bf16[16,128,256]{2,1,0:T(8,128)(2,1)S(1)} collective-permute-done((bf16[16,128,256]{2,1,0:T(8,128)(2,1)}, bf16[16,128,256]{2,1,0:T(8,128)(2,1)S(1)}, u32[]{:S(2)}, u32[]{:S(2)}) %collective-permute-start.3) | collective-permute-done | bytes 1048608 | tf_op jit(solution)/shard_map/cond/branch_1_fun/ppermute | solution.py:263
  28.8 0.0 collective-permute-done.2.received
  28.8 0.4 partner_term.1
  29.2 0.0 collective-permute-done.4.straight
  29.2 0.5 %couple.1 = bf16[16,2,16,256]{3,2,1,0:T(8,128)(2,1)S(1)} custom-call(bf16[256,2048]{1,0:T(8,128)(2,1)S(1)} %get-tuple-element.31.mine, bf16[16,128,256]{2,1,0:T(8,128)(2,1)S(1)} %collective-permute-done.4.straight, f32[256,256]{1,0:T(8,128)S(1)} %get-tuple-element.32.part, bf16[16,16,256]{2,1,0:T(8,128)(2,1)S(1)} %get-tuple-element.33.own), custom_call_target="tpu_custom_call" | custom-call | flops 1000000000 | bytes 6291456 | tf_op jit(solution)/shard_map/couple/pallas_call | solution.py:188
  29.8 18.7 %all_to_all.5 = bf16[32,16,256]{2,1,0:T(8,128)(2,1)S(1)} all-to-all(bf16[32,16,256]{2,1,0:T(8,128)(2,1)S(1)} %bitcast.4), channel_id=1, replica_groups={{0,1,16,17,32,33,48,49,64,65,80,81,96,97,112,113,128,129,144,145,160,16..., dimensions={0} | all-to-all | bytes 524288 | tf_op jit(solution)/shard_map/all_to_all | solution.py:286
  48.5 0.1 collective-permute-start.5
  48.7 1.1 %collective-permute-done.5.given = f32[2,8,256]{2,1,0:T(8,128)S(1)} collective-permute-done((f32[2,8,256]{2,1,0:T(8,128)S(1)}, f32[2,8,256]{2,1,0:T(8,128)S(1)}, u32[]{:S(2)}, u32[]{:S(2)}) %collective-permute-start.5) | collective-permute-done | bytes 16416 | tf_op jit(solution)/shard_map/ppermute | solution.py:288
  49.8 0.6 %finish.1 = f32[8,768]{1,0:T(8,128)} custom-call(f32[2,8,256]{2,1,0:T(8,128)S(1)} %get-tuple-element.34.kept, f32[2,8,256]{2,1,0:T(8,128)S(1)} %collective-permute-done.5.given), custom_call_target="tpu_custom_call" | custom-call | flops 10000 | bytes 100000 | tf_op jit(solution)/shard_map/finish/pallas_call | solution.py:233
  (2 shorter events, 0.0 us)
Async XLA Ops:
  0.0 29.2 %collective-permute-start.4 = (bf16[16,128,256]{2,1,0:T(8,128)(2,1)}, bf16[16,128,256]{2,1,0:T(8,128)(2,1)S(1)}, u32[]{:S(2)}, u32[]{:S(2)}) collective-permute-start(bf16[16,128,256]{2,1,0:T(8,128)(2,1)} %param.11), channel_id=1, source_target_pairs={{0,1},{2,3},{4,5},{6,7},{1,0},{3,2},{5,4},{7,6},{9,10},{11,12},{13... | collective-permute-start | bytes 3145736 | tf_op jit(solution)/shard_map/ppermute | solution.py:256
  0.7 12.6 %collective-permute-start.1 = (bf16[16,128,256]{2,1,0:T(8,128)(2,1)}, bf16[16,128,256]{2,1,0:T(8,128)(2,1)S(1)}, u32[]{:S(2)}, u32[]{:S(2)}) collective-permute-start(bf16[16,128,256]{2,1,0:T(8,128)(2,1)} %get-tuple-element.21.own), channel_id=1, source_target_pairs={{0,8},{16,24},{32,40},{48,56},{64,72},{80,88},{96,104},{112,120},{... | collective-permute-start | bytes 3145736 | tf_op jit(solution)/shard_map/cond/branch_1_fun/ppermute | solution.py:262
  5.4 16.6 %collective-permute-start = (bf16[16,128,256]{2,1,0:T(8,128)(2,1)}, bf16[16,128,256]{2,1,0:T(8,128)(2,1)S(1)}, u32[]{:S(2)}, u32[]{:S(2)}) collective-permute-start(bf16[16,128,256]{2,1,0:T(8,128)(2,1)} %get-tuple-element.21.own), channel_id=1, source_target_pairs={{8,16},{24,32},{40,48},{56,64},{72,80},{88,96},{104,112},{120,128}... | collective-permute-start | bytes 3145736 | tf_op jit(solution)/shard_map/cond/branch_1_fun/ppermute | solution.py:261
  8.4 20.3 %collective-permute-start.3 = (bf16[16,128,256]{2,1,0:T(8,128)(2,1)}, bf16[16,128,256]{2,1,0:T(8,128)(2,1)S(1)}, u32[]{:S(2)}, u32[]{:S(2)}) collective-permute-start(bf16[16,128,256]{2,1,0:T(8,128)(2,1)} %get-tuple-element.21.own), channel_id=1, source_target_pairs={{1,10},{3,12},{5,14},{2,9},{4,11},{6,13},{8,1},{10,3},{12,5},{14,7... | collective-permute-start | bytes 3145736 | tf_op jit(solution)/shard_map/cond/branch_1_fun/ppermute | solution.py:263
  9.8 3.5 %copy-start = (bf16[1,256,128,128]{3,2,1,0:T(8,128)(2,1)S(1)}, bf16[1,256,128,128]{3,2,1,0:T(8,128)(2,1)}, u32[]{:S(2)}) copy-start(bf16[1,256,128,128]{3,2,1,0:T(8,128)(2,1)} %get-tuple-element.43.a_tiles) | copy-start | bytes 25165828 | tf_op jit(solution)/shard_map/cond
  9.8 3.6 %copy-start.1 = (bf16[16,128,256]{2,1,0:T(8,128)(2,1)S(1)}, bf16[16,128,256]{2,1,0:T(8,128)(2,1)}, u32[]{:S(2)}) copy-start(bf16[16,128,256]{2,1,0:T(8,128)(2,1)} %get-tuple-element.21.own) | copy-start | bytes 3145732 | tf_op jit(solution)/shard_map/cond
  24.3 4.4 %collective-permute-start.2 = (bf16[256,2048]{1,0:T(8,128)(2,1)S(1)}, bf16[256,2048]{1,0:T(8,128)(2,1)S(1)}, u32[]{:S(2)}, u32[]{:S(2)}) collective-permute-start(bf16[256,2048]{1,0:T(8,128)(2,1)S(1)} %get-tuple-element.24), channel_id=1, source_target_pairs={{0,8},{16,24},{32,40},{48,56},{64,72},{80,88},{96,104},{112,120},{... | collective-permute-start | bytes 3145736 | tf_op jit(solution)/shard_map/cond/branch_1_fun/ppermute | solution.py:271
  48.5 1.3 %collective-permute-start.5 = (f32[2,8,256]{2,1,0:T(8,128)S(1)}, f32[2,8,256]{2,1,0:T(8,128)S(1)}, u32[]{:S(2)}, u32[]{:S(2)}) collective-permute-start(f32[2,8,256]{2,1,0:T(8,128)S(1)} %get-tuple-element.35), channel_id=1, source_target_pairs={{0,8},{16,24},{32,40},{48,56},{64,72},{80,88},{96,104},{112,120},{... | collective-permute-start | bytes 49160 | tf_op jit(solution)/shard_map/ppermute | solution.py:288
